TPU v7x, 32 devices: a whole 2x2x4 slice. The times are simulated.
32 devices in a mesh: section: 2 (over x), row: 2 (over core), col: 4 (over z), dp: 2 (over y).
Axes of the slice: x: 2, y: 2, z: 4, core: 2. Of those that a mesh axis runs over, the one named last changes fastest.
Arguments:
- inputs: bfloat16 [2, 2, 512, 576], P('dp', None, 'col', 'row'), may hold values from -6 to 6
- segments: int32 [2, 2, 512], P('dp'), may hold values from 0 to 2, as said below
- cotangent: bfloat16 [2, 2, 512, 576], P('dp', None, 'col', 'row'), may hold values from -6 to 6
- gain_attn: bfloat16 [2, 576], P('section', 'row'), may hold values from 0.5 to 1.5
- w_query: bfloat16 [2, 576, 576], P('section', 'row', 'col'), may hold values from -0.25 to 0.25
- w_key: bfloat16 [2, 576, 192], P('section', 'row', 'col'), may hold values from -0.25 to 0.25
- w_value: bfloat16 [2, 576, 192], P('section', 'row', 'col'), may hold values from -0.25 to 0.25
- w_out: bfloat16 [2, 576, 576], P('section', 'col', 'row'), may hold values from -1.5 to 1.5
- gain_ffn: bfloat16 [2, 576], P('section', 'row'), may hold values from 0.5 to 1.5
- w_gate: bfloat16 [2, 576, 1536], P('section', 'row', 'col'), may hold values from -0.25 to 0.25
- w_up: bfloat16 [2, 576, 1536], P('section', 'row', 'col'), may hold values from -0.25 to 0.25
- w_down: bfloat16 [2, 1536, 576], P('section', 'col', 'row'), may hold values from -0.15625 to 0.15625
Outputs:
- activations: bfloat16 [2, 2, 2, 512, 576], P('section', 'dp', None, 'col', 'row')
- input_grads: float32 [2, 2, 2, 512, 576], P('section', 'dp', None, 'col', 'row')
- grad_gain_attn: float32 [2, 576], P('section', 'row')
- grad_w_query: float32 [2, 576, 576], P('section', 'row', 'col')
- grad_w_key: float32 [2, 576, 192], P('section', 'row', 'col')
- grad_w_value: float32 [2, 576, 192], P('section', 'row', 'col')
- grad_w_out: float32 [2, 576, 576], P('section', 'col', 'row')
- grad_gain_ffn: float32 [2, 576], P('section', 'row')
- grad_w_gate: float32 [2, 576, 1536], P('section', 'row', 'col')
- grad_w_up: float32 [2, 576, 1536], P('section', 'row', 'col')
- grad_w_down: float32 [2, 1536, 576], P('section', 'col', 'row')
Inputs may be any that keep to these rules, and one draw needn't show every extreme that they name: `segments`: in each micro-batch the numbers never fall along the sequence and take each of the values 0, 1 and 2 on a run of one or more tokens; the run of 1 starts within the first 64 tokens and ends within the last 64.
All inputs are finite; a program needn't handle non-finite values.
Results may differ from a plain program's by a relative error of at most 0.02.
Values may be sent and summed in bfloat16 or wider, within the bound.
A program may use at most 128 MiB of HBM per device.

v0:
```python
import jax
import jax.numpy as jnp
from jax import lax
from jax.sharding import PartitionSpec as P

D = 576
HEADS = 9
KV_HEADS = 3
HEAD_DIM = 64
MB = 2


EPS = 1e-05
THETA = 100000.0


def for_sending(array):

    def short(part):
        return part.astype(jnp.bfloat16) if part.dtype == jnp.float32 else part

    return jax.tree.map(short, array)


def from_behind(block, axis, distance):
    devices = range(lax.axis_size(axis))
    route = [(i - distance, i) for i in devices if i - distance in devices]
    return lax.ppermute(block, axis, route)


def matmul(left, right):
    return jnp.dot(left, right, preferred_element_type=jnp.float32)


def matmul_tn(left, right):
    return lax.dot_general(
        left, right, (((0,), (0,)), ((), ())), preferred_element_type=jnp.float32
    )


def matmul_nt(left, right):
    return lax.dot_general(
        left, right, (((1,), (1,)), ((), ())), preferred_element_type=jnp.float32
    )


def choose(flag, former, latter):
    return jax.tree.map(lambda left, right: jnp.where(flag, left, right), former, latter)


def narrow_rows(partial_rows):
    return lax.psum_scatter(partial_rows, "row", scatter_dimension=0, tiled=True)


def widen_rows(local_rows):
    return lax.all_gather(local_rows, "row", axis=0, tiled=True)


def grid_gather(items):
    return jax.tree.map(
        lambda part, own: part.astype(own.dtype),
        lax.all_gather(for_sending(items), ("row", "col"), axis=0, tiled=True),
        items,
    )


def grid_sum(items):
    return lax.psum_scatter(items, ("row", "col"), scatter_dimension=0, tiled=True)


def reduce_grads(grads):
    gain_front, w_qkv_grad, w_out_grad, gain_back, w_gate_up_grad, w_down_grad = grads
    gain_front, gain_back = lax.psum((gain_front, gain_back), ("col", "dp"))
    w_qkv_grad, w_out_grad, w_gate_up_grad, w_down_grad = lax.psum(
        (w_qkv_grad, w_out_grad, w_gate_up_grad, w_down_grad), "dp"
    )
    return (gain_front, w_qkv_grad, w_out_grad, gain_back, w_gate_up_grad, w_down_grad)


def norm_local(hidden, gain):
    squares = jnp.sum(hidden * hidden, axis=1, keepdims=True)
    scale = lax.rsqrt(squares / D + EPS)
    return (hidden * scale * gain.astype(jnp.float32)[None, :], scale)


def norm_local_back(hidden, scale, gain, grad_out):
    weighted = grad_out * gain.astype(jnp.float32)[None, :]
    inner = jnp.sum(weighted * hidden, axis=1, keepdims=True)
    grad_hidden = scale * weighted - hidden * (scale * scale * scale) * inner / D
    return (grad_hidden, jnp.sum(grad_out * hidden * scale, axis=0))


def position_tables(segment_row, offset, row_count):
    length = segment_row.shape[0]
    own_ids = lax.dynamic_slice_in_dim(segment_row, offset, row_count)
    token_ids = offset + jnp.arange(row_count, dtype=jnp.int32)
    starts = jnp.sum((segment_row[None, :] < own_ids[:, None]).astype(jnp.int32), axis=1)
    positions = (token_ids - starts).astype(jnp.float32)
    frequency = THETA ** (-jnp.arange(HEAD_DIM // 2, dtype=jnp.float32) * 2.0 / HEAD_DIM)
    angles = positions[:, None] * frequency[None, :]
    angles = jnp.concatenate([angles, angles], axis=1)
    spots = jnp.arange(length, dtype=jnp.int32)
    allowed = (own_ids[:, None] == segment_row[None, :]) & (spots[None, :] <= token_ids[:, None])
    return (jnp.cos(angles), jnp.sin(angles), allowed)


def rotate(vectors, cos_table, sin_table):
    half_dim = vectors.shape[-1] // 2
    turned = jnp.concatenate([-vectors[..., half_dim:], vectors[..., :half_dim]], axis=-1)
    return vectors * cos_table[:, None, :] + turned * sin_table[:, None, :]


def unrotate(grads, cos_table, sin_table):
    half_dim = grads.shape[-1] // 2
    moved = grads * sin_table[:, None, :]
    turned = jnp.concatenate([-moved[..., half_dim:], moved[..., :half_dim]], axis=-1)
    return grads * cos_table[:, None, :] - turned


def split_heads(head_rows, cos_table, sin_table, widths):
    query_cols, key_cols, col_count = widths
    local_rows = head_rows.shape[0]
    head_rows = head_rows.reshape(local_rows, col_count, -1)
    queries = head_rows[:, :, :query_cols].reshape(local_rows, HEADS, HEAD_DIM).astype(jnp.float32)
    key_part = (
        head_rows[:, :, query_cols : query_cols + key_cols]
        .reshape(local_rows, KV_HEADS, HEAD_DIM)
        .astype(jnp.float32)
    )
    value_rows = head_rows[:, :, query_cols + key_cols :].reshape(local_rows, -1)
    query_rot = rotate(queries, cos_table, sin_table).reshape(local_rows, -1).astype(jnp.bfloat16)
    key_rot = rotate(key_part, cos_table, sin_table).reshape(local_rows, -1).astype(jnp.bfloat16)
    return (query_rot, key_rot, value_rows)


def pack_grads(grad_query, grad_keys, grad_values, cos_table, sin_table, widths):
    query_cols, key_cols, col_count = widths
    local_rows = grad_query.shape[0]
    grad_q = unrotate(grad_query, cos_table, sin_table).reshape(local_rows, col_count, query_cols)
    grad_k = unrotate(
        grad_keys.reshape(local_rows, KV_HEADS, HEAD_DIM), cos_table, sin_table
    ).reshape(local_rows, col_count, key_cols)
    grad_v = grad_values.reshape(local_rows, col_count, key_cols)
    return (
        jnp.concatenate([grad_q, grad_k, grad_v], axis=2)
        .reshape(local_rows, -1)
        .astype(jnp.bfloat16)
    )


def head_scores(queries, key_rows, allowed):
    query_rows = queries.shape[0]
    grouped = queries.reshape(query_rows, KV_HEADS, HEADS // KV_HEADS, HEAD_DIM)
    key_heads = key_rows.reshape(key_rows.shape[0], KV_HEADS, HEAD_DIM)
    scores = jnp.einsum(
        "qhgd,khd->hgqk", grouped, key_heads, preferred_element_type=jnp.float32
    ) * HEAD_DIM ** (-0.5)
    return (jnp.where(allowed[None, None], scores, -1e30), grouped, key_heads)


def attend(queries, key_rows, value_rows, allowed):
    scores, grouped, key_heads = head_scores(queries, key_rows, allowed)
    highest = jnp.max(scores, axis=3, keepdims=True)
    logsum = highest + jnp.log(jnp.sum(jnp.exp(scores - highest), axis=3, keepdims=True))
    weights = jnp.exp(scores - logsum).astype(jnp.bfloat16)
    value_heads = value_rows.reshape(value_rows.shape[0], KV_HEADS, HEAD_DIM)
    output = jnp.einsum("hgqk,khd->qhgd", weights, value_heads, preferred_element_type=jnp.float32)
    return (output.reshape(queries.shape[0], -1), logsum)


def attend_back(queries, key_rows, value_rows, allowed, logsum, grad_out):
    scores, grouped, key_heads = head_scores(queries, key_rows, allowed)
    weights = jnp.exp(scores - logsum)
    value_heads = value_rows.reshape(value_rows.shape[0], KV_HEADS, HEAD_DIM)
    grad_heads = grad_out.reshape(grouped.shape)
    grad_weights = jnp.einsum(
        "qhgd,khd->hgqk", grad_heads, value_heads, preferred_element_type=jnp.float32
    )
    inner = jnp.sum(grad_weights * weights, axis=3, keepdims=True)
    grad_scores = (weights * (grad_weights - inner)).astype(jnp.bfloat16)
    factor = HEAD_DIM ** (-0.5)
    grad_query = (
        jnp.einsum("hgqk,khd->qhgd", grad_scores, key_heads, preferred_element_type=jnp.float32)
        * factor
    )
    grad_key = (
        jnp.einsum("hgqk,qhgd->khd", grad_scores, grouped, preferred_element_type=jnp.float32)
        * factor
    )
    grad_value = jnp.einsum(
        "hgqk,qhgd->khd",
        weights.astype(jnp.bfloat16),
        grad_heads,
        preferred_element_type=jnp.float32,
    )
    key_count = key_rows.shape[0]
    return (
        grad_query.reshape(queries.shape[0], HEADS, HEAD_DIM),
        grad_key.reshape(key_count, -1),
        grad_value.reshape(key_count, -1),
    )


def gather_ordered(key_rot, value_rows):
    row_parts = lax.axis_size("row")
    col_parts = lax.axis_size("col")
    rows = key_rot.shape[0]
    all_keys, all_values = grid_gather((key_rot, value_rows))

    def reorder(block):
        return (
            block.reshape(row_parts, col_parts, rows, block.shape[1])
            .transpose(1, 0, 2, 3)
            .reshape(-1, block.shape[1])
        )

    return (reorder(all_keys), reorder(all_values))


def scatter_ordered(grad_keys_all, grad_values_all):
    row_parts = lax.axis_size("row")
    col_parts = lax.axis_size("col")
    rows = grad_keys_all.shape[0] // (row_parts * col_parts)

    def reorder(block):
        return (
            block.reshape(col_parts, row_parts, rows, block.shape[1])
            .transpose(1, 0, 2, 3)
            .reshape(-1, block.shape[1])
        )

    return grid_sum((reorder(grad_keys_all), reorder(grad_values_all)))


def assemble(weights):
    gain_attn, w_qkv, w_out, gain_ffn, w_gate_up, w_down = weights
    row_parts = lax.axis_size("row")
    col_parts = lax.axis_size("col")
    qkv_all, out_all, gate_up_all, down_all, attn_gain_all, ffn_gain_all = grid_gather(
        (w_qkv, w_out, w_gate_up, w_down, gain_attn, gain_ffn)
    )
    band, qkv_width = w_qkv.shape
    qkv_full = (
        qkv_all.reshape(row_parts, col_parts, band, qkv_width)
        .transpose(0, 2, 1, 3)
        .reshape(row_parts * band, col_parts * qkv_width)
    )
    out_rows, out_width = w_out.shape
    out_full = (
        out_all.reshape(row_parts, col_parts, out_rows, out_width)
        .transpose(1, 2, 0, 3)
        .reshape(col_parts * out_rows, row_parts * out_width)
    )
    ffn_cols = w_gate_up.shape[1] // 2
    gate_up_full = (
        gate_up_all.reshape(row_parts, col_parts, band, 2, ffn_cols)
        .transpose(0, 2, 3, 1, 4)
        .reshape(row_parts * band, 2 * col_parts * ffn_cols)
    )
    down_rows, down_width = w_down.shape
    down_full = (
        down_all.reshape(row_parts, col_parts, down_rows, down_width)
        .transpose(1, 2, 0, 3)
        .reshape(col_parts * down_rows, row_parts * down_width)
    )
    gain_len = gain_attn.shape[0]
    attn_gain_full = attn_gain_all.reshape(row_parts, col_parts, gain_len)[:, 0].reshape(-1)
    ffn_gain_full = ffn_gain_all.reshape(row_parts, col_parts, gain_len)[:, 0].reshape(-1)
    return (attn_gain_full, qkv_full, out_full, ffn_gain_full, gate_up_full, down_full)


def to_grid(grads):
    grad_gain_a, grad_qkv, grad_out, grad_gain_f, grad_gate_up, grad_down = grads
    row_parts = lax.axis_size("row")
    col_parts = lax.axis_size("col")
    width = grad_qkv.shape[0]
    band = width // row_parts
    qkv_width = grad_qkv.shape[1] // col_parts
    qkv_grid = (
        grad_qkv.reshape(row_parts, band, col_parts, qkv_width)
        .transpose(0, 2, 1, 3)
        .reshape(-1, qkv_width)
    )
    out_grid = (
        grad_out.reshape(col_parts, width // col_parts, row_parts, band)
        .transpose(2, 0, 1, 3)
        .reshape(-1, band)
    )
    ffn_cols = grad_gate_up.shape[1] // (2 * col_parts)
    gate_up_grid = (
        grad_gate_up.reshape(row_parts, band, 2, col_parts, ffn_cols)
        .transpose(0, 3, 1, 2, 4)
        .reshape(-1, 2 * ffn_cols)
    )
    hidden_units = grad_down.shape[0]
    down_grid = (
        grad_down.reshape(col_parts, hidden_units // col_parts, row_parts, band)
        .transpose(2, 0, 1, 3)
        .reshape(-1, band)
    )
    picked = (jnp.arange(col_parts, dtype=jnp.int32) == lax.axis_index("col")).astype(jnp.float32)

    def spread(gain_grad):
        return (gain_grad.reshape(row_parts, 1, band) * picked[None, :, None]).reshape(-1)

    return grid_sum(
        (spread(grad_gain_a), qkv_grid, out_grid, spread(grad_gain_f), gate_up_grid, down_grid)
    )


def to_rows(grid_block):
    row_parts = lax.axis_size("row")
    tokens, band = grid_block.shape
    stacked = widen_rows(grid_block)
    whole = (
        stacked.reshape(row_parts, tokens, band)
        .transpose(1, 0, 2)
        .reshape(tokens, row_parts * band)
    )
    rows = tokens // row_parts
    return lax.dynamic_slice_in_dim(whole, lax.axis_index("row") * rows, rows, 0)


def from_rows(row_block):
    row_parts = lax.axis_size("row")
    band = row_block.shape[1] // row_parts
    stacked = widen_rows(row_block)
    return lax.dynamic_slice_in_dim(stacked, lax.axis_index("row") * band, band, 1)


def grads_to_grid(row_block):
    row_parts = lax.axis_size("row")
    rows, width = row_block.shape
    band = width // row_parts
    pieces = row_block.reshape(rows, row_parts, band).transpose(1, 0, 2)
    picked = (jnp.arange(row_parts, dtype=jnp.int32) == lax.axis_index("row")).astype(jnp.float32)
    placed = pieces[:, None] * picked[None, :, None, None]
    return narrow_rows(placed.reshape(row_parts * row_parts * rows, band))


def rows_forward(entry, full, table_set, widths):
    gain_attn, w_qkv, w_out, gain_ffn, w_gate_up, w_down = full
    cos_table, sin_table, allowed = table_set
    normed, scale_attn = norm_local(entry, gain_attn)
    normed_b = normed.astype(jnp.bfloat16)
    projected = matmul(normed_b, w_qkv).astype(jnp.bfloat16)
    query_rot, key_rot, value_rows = split_heads(projected, cos_table, sin_table, widths)
    all_keys, all_values = gather_ordered(key_rot, value_rows)
    attended, logsum = attend(query_rot, all_keys, all_values, allowed)
    attended_b = attended.astype(jnp.bfloat16)
    residual = entry + matmul(attended_b, w_out)
    normed_ffn, scale_ffn = norm_local(residual, gain_ffn)
    normed_ffn_b = normed_ffn.astype(jnp.bfloat16)
    gate_up = matmul(normed_ffn_b, w_gate_up)
    split_at = w_down.shape[0]
    gate_vals = gate_up[:, :split_at]
    up_vals = gate_up[:, split_at:]
    inner_b = (jax.nn.silu(gate_vals) * up_vals).astype(jnp.bfloat16)
    result = residual + matmul(inner_b, w_down)
    key_keep = (all_keys, all_values)
    saved = (
        entry,
        scale_attn,
        normed_b,
        query_rot,
        key_keep[0],
        key_keep[1],
        logsum,
        attended_b,
        residual,
        scale_ffn,
        normed_ffn_b,
        gate_vals,
        up_vals,
        inner_b,
    )
    return (result, saved)


def rows_backward(grad_out, saved, full, table_set, widths):
    gain_attn, w_qkv, w_out, gain_ffn, w_gate_up, w_down = full
    cos_table, sin_table, allowed = table_set
    (
        entry,
        scale_attn,
        normed_b,
        query_rot,
        key_first,
        key_second,
        logsum,
        attended_b,
        residual,
        scale_ffn,
        normed_ffn_b,
        gate_vals,
        up_vals,
        inner_b,
    ) = saved
    all_keys, all_values = (key_first, key_second)
    grad_b = grad_out.astype(jnp.bfloat16)
    grad_w_down = matmul_tn(inner_b, grad_b)
    grad_inner = matmul_nt(grad_b, w_down)
    sigmoid_vals = jax.nn.sigmoid(gate_vals)
    grad_gate = grad_inner * up_vals * (sigmoid_vals * (1.0 + gate_vals * (1.0 - sigmoid_vals)))
    grad_up = grad_inner * (gate_vals * sigmoid_vals)
    grad_gate_up = jnp.concatenate([grad_gate, grad_up], axis=1).astype(jnp.bfloat16)
    grad_w_gate_up = matmul_tn(normed_ffn_b, grad_gate_up)
    grad_normed_ffn = matmul_nt(grad_gate_up, w_gate_up)
    grad_norm_ffn, grad_gain_ffn = norm_local_back(residual, scale_ffn, gain_ffn, grad_normed_ffn)
    grad_residual = grad_out + grad_norm_ffn
    grad_res_b = grad_residual.astype(jnp.bfloat16)
    grad_w_out = matmul_tn(attended_b, grad_res_b)
    grad_attended = matmul_nt(grad_res_b, w_out).astype(jnp.bfloat16)
    grad_query, grad_keys_all, grad_values_all = attend_back(
        query_rot, all_keys, all_values, allowed, logsum, grad_attended
    )
    grad_keys, grad_values = scatter_ordered(grad_keys_all, grad_values_all)
    packed = pack_grads(grad_query, grad_keys, grad_values, cos_table, sin_table, widths)
    grad_w_qkv = matmul_tn(normed_b, packed)
    grad_normed = matmul_nt(packed, w_qkv)
    grad_norm_attn, grad_gain_attn = norm_local_back(entry, scale_attn, gain_attn, grad_normed)
    grad_entry = grad_residual + grad_norm_attn
    return (
        grad_entry,
        (grad_gain_attn, grad_w_qkv, grad_w_out, grad_gain_ffn, grad_w_gate_up, grad_w_down),
    )


def on_device(
    inputs,
    segments,
    cotangent,
    gain_attn,
    w_query,
    w_key,
    w_value,
    w_out,
    gain_ffn,
    w_gate,
    w_up,
    w_down,
):
    front_section = lax.axis_index("section") == 0
    col_count = lax.axis_size("col")
    query_cols = w_query.shape[2]
    key_cols = w_key.shape[2]
    widths = (query_cols, key_cols, col_count)
    w_qkv = jnp.concatenate([w_query[0], w_key[0], w_value[0]], axis=1)
    w_gate_up = jnp.concatenate([w_gate[0], w_up[0]], axis=1)
    weights = (gain_attn[0], w_qkv, w_out[0], gain_ffn[0], w_gate_up, w_down[0])
    seq_len = segments.shape[2]
    row_count = seq_len // (lax.axis_size("row") * col_count)
    full = assemble(weights)
    place = lax.axis_index("col") * lax.axis_size("row") + lax.axis_index("row")
    table_list = [
        position_tables(segments[0, batch_no], place * row_count, row_count)
        for batch_no in range(MB)
    ]
    carried = jnp.zeros(inputs.shape[2:], jnp.bfloat16)
    outs_by_moment = []
    saved_by_moment = []
    for moment in range(MB + 1):
        mine = min(moment, MB - 1)
        theirs = max(moment - 1, 0)
        entry = jnp.where(front_section, inputs[0, mine], carried)
        table_set = choose(front_section, table_list[mine], table_list[theirs])
        result, saved = rows_forward(to_rows(entry).astype(jnp.float32), full, table_set, widths)
        result_b = from_rows(result.astype(jnp.bfloat16))
        outs_by_moment.append(result_b)
        saved_by_moment.append(saved)
        if moment < MB:
            carried = from_behind(result_b, "section", 1)
    grad_in = jnp.zeros(inputs.shape[2:], jnp.bfloat16)
    totals = tuple((jnp.zeros(item.shape, jnp.float32) for item in full))
    grads_by_moment = []
    for moment in range(MB + 1):
        late = min(moment, MB - 1)
        early = max(moment - 1, 0)
        seed_grad = jnp.where(front_section, grad_in, cotangent[0, late])
        saved = choose(front_section, saved_by_moment[early], saved_by_moment[min(moment + 1, MB)])
        table_set = choose(front_section, table_list[early], table_list[late])
        grad_rows, grads = rows_backward(
            to_rows(seed_grad).astype(jnp.float32), saved, full, table_set, widths
        )
        grad_entry = grads_to_grid(grad_rows)
        is_valid = jnp.where(front_section, moment >= 1, moment < MB)
        masked = tuple((jnp.where(is_valid, item, 0.0) for item in grads))
        totals = tuple((left + right for left, right in zip(totals, masked)))
        grads_by_moment.append(grad_entry)
        if moment < MB:
            grad_in = from_behind(grad_entry.astype(jnp.bfloat16), "section", -1)
    totals = reduce_grads(to_grid(totals))
    activations = jnp.stack(
        [
            jnp.where(front_section, outs_by_moment[batch_no], outs_by_moment[batch_no + 1])
            for batch_no in range(MB)
        ]
    )[None, None]
    input_grads = jnp.stack(
        [
            jnp.where(front_section, grads_by_moment[batch_no + 1], grads_by_moment[batch_no])
            for batch_no in range(MB)
        ]
    )[None, None]
    grad_gain_attn, grad_w_qkv, grad_w_out, grad_gain_ffn, grad_w_gate_up, grad_w_down = totals
    grad_w_query = grad_w_qkv[:, :query_cols]
    grad_w_key = grad_w_qkv[:, query_cols : query_cols + key_cols]
    grad_w_value = grad_w_qkv[:, query_cols + key_cols :]
    split_at = w_down.shape[1]
    grad_w_gate = grad_w_gate_up[:, :split_at]
    grad_w_up = grad_w_gate_up[:, split_at:]
    return (
        activations,
        input_grads,
        grad_gain_attn[None],
        grad_w_query[None],
        grad_w_key[None],
        grad_w_value[None],
        grad_w_out[None],
        grad_gain_ffn[None],
        grad_w_gate[None],
        grad_w_up[None],
        grad_w_down[None],
    )


def solution(mesh):
    placed = (
        P("dp", None, "col", "row"),
        P("dp", None, None),
        P("dp", None, "col", "row"),
        P("section", "row"),
        P("section", "row", "col"),
        P("section", "row", "col"),
        P("section", "row", "col"),
        P("section", "col", "row"),
        P("section", "row"),
        P("section", "row", "col"),
        P("section", "row", "col"),
        P("section", "col", "row"),
    )
    return jax.shard_map(
        on_device,
        mesh=mesh,
        in_specs=placed,
        out_specs=(
            P("section", "dp", None, "col", "row"),
            P("section", "dp", None, "col", "row"),
            P("section", "row"),
            P("section", "row", "col"),
            P("section", "row", "col"),
            P("section", "row", "col"),
            P("section", "col", "row"),
            P("section", "row"),
            P("section", "row", "col"),
            P("section", "row", "col"),
            P("section", "col", "row"),
        ),
        check_vma=False,
    )
```

profile of v0, /device:TPU:0, one launch (start us, length us, event | category | flops | bytes accessed | tf_op | source)
XLA Modules:
  0.0 1108.8 jit_solution(3077625105907558559)
XLA Ops:
  16.9 31.0 %all-reduce.7 = (bf16[2304]{0:T(1024)(128)(2,1)S(1)}, bf16[2304]{0:T(1024)(128)(2,1)S(1)}) all-reduce(bf16[2304]{0:T(1024)(128)(2,1)S(1)} %dynamic-update-slice, bf16[2304]{0:T(1024)(128)(2,1)S(1)} %dynamic-update-slice.1), channel_id=3, replica_groups=mesh['section'=2,'row'=2,'col'=4,'dp'=2] {'row','col'}, use_global_device_ids=true, to_apply=%add | all-reduce | flops 4608 | bytes 18432
  48.1 34.4 %all-gather.2 = bf16[1,1152,288]{2,1,0:T(8,128)(2,1)S(1)} all-gather(bf16[1,144,288]{2,1,0:T(8,128)(2,1)S(1)} %copy-done.141), channel_id=4, replica_groups=mesh['section'=2,'row'=2,'col'=4,'dp'=2] {'row','col'}, dimensions={1}, use_global_device_ids=true | all-gather | bytes 746496 | tf_op jit(solution)/shard_map/all_gather | solution.py:62
  91.8 2.2 copy.237
  96.2 26.5 %all_gather.67 = bf16[512,192]{1,0:T(8,128)(2,1)S(1)} all-gather(bf16[64,192]{1,0:T(8,128)(2,1)S(1)} %copy.242), channel_id=1, replica_groups=mesh['section'=2,'row'=2,'col'=4,'dp'=2] {'row','col'}, dimensions={0}, use_global_device_ids=true | all-gather | bytes 221184 | tf_op jit(solution)/shard_map/all_gather | solution.py:62
  123.6 25.4 %all_gather.66 = bf16[512,192]{1,0:T(8,128)(2,1)S(1)} all-gather(bf16[64,192]{1,0:T(8,128)(2,1)S(1)} %copy.239), channel_id=1, replica_groups=mesh['section'=2,'row'=2,'col'=4,'dp'=2] {'row','col'}, dimensions={0}, use_global_device_ids=true | all-gather | bytes 221184 | tf_op jit(solution)/shard_map/all_gather | solution.py:62
  153.0 3.5 reshape.1178
  158.7 6.6 reshape.1176
  165.3 6.4 copy.355
  171.7 5.6 reshape.1177
  182.6 4.3 collective-permute-start
  192.4 2.1 all_gather.73
  201.6 2.4 convolution_convert_fusion.4
  212.5 27.4 %all_gather.75 = bf16[512,192]{1,0:T(8,128)(2,1)} all-gather(bf16[64,192]{1,0:T(8,128)(2,1)} %copy.256), channel_id=1, replica_groups=mesh['section'=2,'row'=2,'col'=4,'dp'=2] {'row','col'}, dimensions={0}, use_global_device_ids=true | all-gather | bytes 221184 | tf_op jit(solution)/shard_map/all_gather | solution.py:62
  251.6 27.4 %all_gather.74 = bf16[512,192]{1,0:T(8,128)(2,1)} all-gather(bf16[64,192]{1,0:T(8,128)(2,1)} %copy.253), channel_id=1, replica_groups=mesh['section'=2,'row'=2,'col'=4,'dp'=2] {'row','col'}, dimensions={0}, use_global_device_ids=true | all-gather | bytes 221184 | tf_op jit(solution)/shard_map/all_gather | solution.py:62
  292.9 2.3 collective-permute-start.1
  299.6 2.1 all_gather.77
  309.5 2.4 convolution_convert_fusion.3
  319.1 27.4 %all_gather.79 = bf16[512,192]{1,0:T(8,128)(2,1)} all-gather(bf16[64,192]{1,0:T(8,128)(2,1)} %copy.266), channel_id=1, replica_groups=mesh['section'=2,'row'=2,'col'=4,'dp'=2] {'row','col'}, dimensions={0}, use_global_device_ids=true | all-gather | bytes 221184 | tf_op jit(solution)/shard_map/all_gather | solution.py:62
  357.2 27.9 %all_gather.78 = bf16[512,192]{1,0:T(8,128)(2,1)} all-gather(bf16[64,192]{1,0:T(8,128)(2,1)} %copy.263), channel_id=1, replica_groups=mesh['section'=2,'row'=2,'col'=4,'dp'=2] {'row','col'}, dimensions={0}, use_global_device_ids=true | all-gather | bytes 221184 | tf_op jit(solution)/shard_map/all_gather | solution.py:62
  389.0 2.7 broadcast_select_fusion.3
  402.6 2.4 reshape_reshape.42
  405.1 2.1 copy.275
  407.2 2.4 convolution_bitcast_fusion.7
  409.6 2.4 reshape_reshape.43
  412.0 2.1 copy.278
  420.7 18.7 %reduce-scatter.14.cloned.1.call-done = f32[64,192]{1,0:T(8,128)} async-done(((f32[512,192]{1,0:T(8,128)}), f32[64,192]{1,0:T(8,128)}) %reduce-scatter.14.cloned.1.call-update) | async-done | bytes 49168 | tf_op jit(solution)/shard_map/reduce_scatter | solution.py:68
  444.2 28.8 %reduce-scatter.16.cloned.1.call-done = f32[64,192]{1,0:T(8,128)} async-done(((f32[512,192]{1,0:T(8,128)}), f32[64,192]{1,0:T(8,128)}) %reduce-scatter.16.cloned.1.call-update) | async-done | bytes 49168 | tf_op jit(solution)/shard_map/reduce_scatter | solution.py:68
  476.3 2.4 multiply_reduce_fusion.8
  488.7 2.6 fusion.137
  494.2 2.5 fusion.7
  501.1 2.1 all_gather.82
  508.3 2.5 multiply_convert_fusion.6
  520.2 2.4 reshape_reshape.44
  522.7 2.1 copy.287
  525.0 2.4 convolution_bitcast_fusion.5
  527.4 2.4 reshape_reshape.45
  529.8 2.1 copy.290
  538.5 20.3 %reduce-scatter.20.cloned.1.call-done = f32[64,192]{1,0:T(8,128)} async-done(((f32[512,192]{1,0:T(8,128)}), f32[64,192]{1,0:T(8,128)}) %reduce-scatter.20.cloned.1.call-update) | async-done | bytes 49168 | tf_op jit(solution)/shard_map/reduce_scatter | solution.py:68
  563.6 28.8 %reduce-scatter.22.cloned.1.call-done = f32[64,192]{1,0:T(8,128)} async-done(((f32[512,192]{1,0:T(8,128)}), f32[64,192]{1,0:T(8,128)}) %reduce-scatter.22.cloned.1.call-update) | async-done | bytes 49168 | tf_op jit(solution)/shard_map/reduce_scatter | solution.py:68
  602.7 2.5 fusion.3
  605.2 4.2 reduce-scatter.24.cloned.1.call-done
  611.7 2.4 fusion.99
  614.1 3.0 collective-permute-done.3
  617.2 2.1 all_gather.83
  622.7 3.3 multiply_convert_fusion.4
  627.7 3.0 multiply_reduce_fusion.3
  642.4 3.4 reshape.1227
  645.8 2.9 copy.305
  650.8 16.3 %reduce-scatter.28.cloned.1.call-done = f32[64,192]{1,0:T(8,128)} async-done(((f32[512,192]{1,0:T(8,128)}), f32[64,192]{1,0:T(8,128)}) %reduce-scatter.28.cloned.1.call-update) | async-done | bytes 49168 | tf_op jit(solution)/shard_map/reduce_scatter | solution.py:68
  668.1 32.9 %reduce-scatter.26.cloned.1.call-done = f32[64,192]{1,0:T(8,128)} async-done(((f32[512,192]{1,0:T(8,128)}), f32[64,192]{1,0:T(8,128)}) %reduce-scatter.26.cloned.1.call-update) | async-done | bytes 49168 | tf_op jit(solution)/shard_map/reduce_scatter | solution.py:68
  705.8 3.5 reshape.1225
  715.0 2.9 reshape.1231
  717.9 2.6 copy.307
  720.5 3.0 reshape.1232
  726.9 4.3 select_add_fusion
  731.2 9.6 reshape.1229
  740.8 9.5 copy.306
  750.3 6.6 copy.352
  760.2 40.3 %reduce-scatter.32.cloned.1.call-done = f32[288,240]{1,0:T(8,128)} async-done(((f32[2304,240]{1,0:T(8,128)}), f32[288,240]{1,0:T(8,128)}) %reduce-scatter.32.cloned.1.call-update) | async-done | bytes 276496 | tf_op jit(solution)/shard_map/reduce_scatter | solution.py:68
  800.5 77.3 %reduce-scatter.38.cloned.1.call-done = f32[384,288]{0,1:T(8,128)} async-done(((f32[3072,288]{0,1:T(8,128)}), f32[384,288]{0,1:T(8,128)}) %reduce-scatter.38.cloned.1.call-update) | async-done | bytes 442384 | tf_op jit(solution)/shard_map/reduce_scatter | solution.py:68
  877.8 144.3 %reduce-scatter.36.cloned.1.call-done = f32[288,768]{1,0:T(8,128)} async-done(((f32[2304,768]{1,0:T(8,128)}), f32[288,768]{1,0:T(8,128)}) %reduce-scatter.36.cloned.1.call-update) | async-done | bytes 884752 | tf_op jit(solution)/shard_map/reduce_scatter | solution.py:68
  1027.9 28.4 %all-reduce.5 = (f32[2304]{0:T(1024)S(1)}, f32[2304]{0:T(1024)S(1)}) all-reduce(f32[2304]{0:T(1024)S(1)} %mul.1229, f32[2304]{0:T(1024)S(1)} %mul.1238), channel_id=17, replica_groups=mesh['section'=2,'row'=2,'col'=4,'dp'=2] {'row','col'}, use_global_device_ids=true, to_apply=%region_35.36.clone | all-reduce | flops 4608 | bytes 36864
  1056.4 19.4 %all-reduce.4 = (f32[1,288]{1,0:T(1,128)}, f32[1,288]{1,0:T(1,128)}) all-reduce(f32[1,288]{1,0:T(1,128)S(1)} %broadcast_in_dim.101, f32[1,288]{1,0:T(1,128)S(1)} %broadcast_in_dim.108), channel_id=1, replica_groups=mesh['section'=2,'row'=2,'col'=4,'dp'=2] {'col','dp'}, use_global_device_ids=true, to_apply=%region_36.37 | all-reduce | flops 576 | bytes 4608 | tf_op jit(solution)/shard_map/psum | solution.py:73
  1077.7 17.4 %all-reduce.10.cloned.1.call-done = (f32[288,240]{1,0:T(8,128)}, f32[1,144,288]{2,1,0:T(8,128)}, f32[288,768]{1,0:T(8,128)}, f32[1,384,288]{1,2,0:T(8,128)}) async-done(((f32[288,240]{1,0:T(8,128)}, f32[1,144,288]{2,1,0:T(8,128)}, f32[288,768]{1,0:T(8,128)}, f32[1,384,288]{1,2,0:T(8,128)}), (f32[288,240]{1,0:T(8,128)}, f32[1,144,288]{2,1,0:T(8,128)}, f32[288,768]{1,0:T(8,128)}, ...) | async-done | bytes 1769488 | tf_op jit(solution)/shard_map/psum | solution.py:74
  (669 shorter events, 244.5 us)
Async XLA Ops:
  7.2 4.6 copy-start.130
  7.2 4.6 copy-start.131
  7.2 84.6 %all-gather.10.cloned.1.call-start = ((), (), s32[]{:S(2)}) async-start(), calls=%async_computation.13 | async-start | bytes 1327104 | tf_op jit(solution)/shard_map/all_gather | solution.py:62
  11.0 142.0 %all-gather.14.cloned.1.call-start = ((), (), s32[]{:S(2)}) async-start(), calls=%async_computation.28 | async-start | bytes 1990656 | tf_op jit(solution)/shard_map/all_gather | solution.py:62
  11.7 147.0 %all-gather.12.cloned.1.call-start = ((), (), s32[]{:S(2)}) async-start(), calls=%async_computation.14 | async-start | bytes 3981312 | tf_op jit(solution)/shard_map/all_gather | solution.py:62
  12.6 35.5 %copy-start.141 = (bf16[1,144,288]{2,1,0:T(8,128)(2,1)S(1)}, bf16[1,144,288]{2,1,0:T(8,128)(2,1)}, u32[]{:S(2)}) copy-start(bf16[1,144,288]{2,1,0:T(8,128)(2,1)} %param.19) | copy-start | bytes 248836
  12.6 426.8 %reduce-scatter.14.cloned.1.call-start = ((), (), s32[]{:S(2)}) async-start(), calls=%async_computation.15 | async-start | bytes 589824 | tf_op jit(solution)/shard_map/reduce_scatter | solution.py:68
  15.1 136.8 %copy-start.15 = (bf16[64,576]{1,0:T(8,128)(2,1)}, bf16[64,576]{1,0:T(8,128)(2,1)S(1)}, u32[]{:S(2)}) copy-start(bf16[64,576]{1,0:T(8,128)(2,1)S(1)} %copy.343) | copy-start | bytes 221188
  84.0 67.8 %copy-start.2 = (bf16[576,576]{1,0:T(8,128)(2,1)}, bf16[576,576]{1,0:T(8,128)(2,1)S(1)}, u32[]{:S(2)}) copy-start(bf16[576,576]{1,0:T(8,128)(2,1)S(1)} %reshape.1174) | copy-start | bytes 1990660
  84.0 5.2 copy-start.159
  87.8 4.1 copy-start.91
  89.9 4.1 copy-start.133
  90.0 59.9 %copy-start.102 = (f32[64,64]{0,1:T(8,128)}, f32[64,64]{0,1:T(8,128)S(1)}, u32[]{:S(2)}) copy-start(f32[64,64]{0,1:T(8,128)S(1)} %fusion.103) | copy-start | bytes 49156
  90.9 59.0 %copy-start.98 = (f32[64,64]{0,1:T(8,128)}, f32[64,64]{0,1:T(8,128)S(1)}, u32[]{:S(2)}) copy-start(f32[64,64]{0,1:T(8,128)S(1)} %get-tuple-element.153) | copy-start | bytes 49156
  91.0 4.1 copy-start.153
  123.2 26.6 %copy-start.39 = (bf16[4,2,64,192]{2,1,0,3:T(2,128)(2,1)}, bf16[4,2,64,192]{2,1,0,3:T(2,128)(2,1)S(1)}, u32[]{:S(2)}) copy-start(bf16[4,2,64,192]{2,1,0,3:T(2,128)(2,1)S(1)} %copy.243) | copy-start | bytes 589828
  179.2 7.6 copy-start.134
  182.6 8.9 collective-permute-start
  285.1 4.3 copy-start.33
  289.5 5.7 copy-start.57
  289.5 5.7 copy-start.61
  289.5 5.7 copy-start.77
  289.5 5.7 copy-start.79
  289.5 5.7 copy-start.139
  289.5 5.7 copy-start.151
  292.9 5.7 collective-permute-start.1
  388.9 3.8 copy-start.34
  388.9 3.8 copy-start.37
  388.9 3.8 copy-start.112
  407.2 65.8 %reduce-scatter.16.cloned.1.call-start = ((), (), s32[]{:S(2)}) async-start(), calls=%async_computation.16 | async-start | bytes 589824 | tf_op jit(solution)/shard_map/reduce_scatter | solution.py:68
  417.2 74.1 %reduce-scatter.18.cloned.1.call-start = ((), (), s32[]{:S(2)}) async-start(), calls=%async_computation.17 | async-start | bytes 589824 | tf_op jit(solution)/shard_map/reduce_scatter | solution.py:52
  474.5 4.2 copy-start.16
  474.5 4.2 copy-start.24
  474.5 4.2 copy-start.50
  484.4 74.3 %reduce-scatter.20.cloned.1.call-start = ((), (), s32[]{:S(2)}) async-start(), calls=%async_computation.18 | async-start | bytes 589824 | tf_op jit(solution)/shard_map/reduce_scatter | solution.py:68
  488.7 5.5 copy-start.150
  492.9 7.3 collective-permute-start.2
  524.8 67.6 %reduce-scatter.22.cloned.1.call-start = ((), (), s32[]{:S(2)}) async-start(), calls=%async_computation.19 | async-start | bytes 589824 | tf_op jit(solution)/shard_map/reduce_scatter | solution.py:68
  535.0 74.5 %reduce-scatter.24.cloned.1.call-start = ((), (), s32[]{:S(2)}) async-start(), calls=%async_computation.20 | async-start | bytes 589824 | tf_op jit(solution)/shard_map/reduce_scatter | solution.py:52
  595.7 6.1 copy-start.143
  602.7 64.5 %reduce-scatter.28.cloned.1.call-start = ((), (), s32[]{:S(2)}) async-start(), calls=%async_computation.22 | async-start | bytes 589824 | tf_op jit(solution)/shard_map/reduce_scatter | solution.py:68
  609.4 7.8 copy-start.95
  610.4 6.8 collective-permute-start.3
  630.8 9.1 copy-start.54
  634.2 66.9 %reduce-scatter.26.cloned.1.call-start = ((), (), s32[]{:S(2)}) async-start(), calls=%async_computation.21 | async-start | bytes 589824 | tf_op jit(solution)/shard_map/reduce_scatter | solution.py:68
  637.8 122.3 %reduce-scatter.34.cloned.1.call-start = ((), (), s32[]{:S(2)}) async-start(), calls=%async_computation.25 | async-start | bytes 1990656 | tf_op jit(solution)/shard_map/reduce_scatter | solution.py:68
  648.7 151.8 %reduce-scatter.32.cloned.1.call-start = ((), (), s32[]{:S(2)}) async-start(), calls=%async_computation.24 | async-start | bytes 2654208 | tf_op jit(solution)/shard_map/reduce_scatter | solution.py:68
  650.8 52.0 %copy-start.21 = (bf16[64,576]{1,0:T(8,128)(2,1)S(1)}, bf16[64,576]{1,0:T(8,128)(2,1)}, u32[]{:S(2)}) copy-start(bf16[64,576]{1,0:T(8,128)(2,1)} %copy.346) | copy-start | bytes 221188
  650.8 52.0 %copy-start.149 = (f32[64]{0:T(128)S(1)}, f32[64]{0:T(128)}, u32[]{:S(2)}) copy-start(f32[64]{0:T(128)} %copy-done.148) | copy-start | bytes 772
  711.3 166.5 %reduce-scatter.38.cloned.1.call-start = ((), (), s32[]{:S(2)}) async-start(), calls=%async_computation.27 | async-start | bytes 3981312 | tf_op jit(solution)/shard_map/reduce_scatter | solution.py:68
  723.6 298.5 %reduce-scatter.36.cloned.1.call-start = ((), (), s32[]{:S(2)}) async-start(), calls=%async_computation.26 | async-start | bytes 7962624 | tf_op jit(solution)/shard_map/reduce_scatter | solution.py:68
  757.0 318.9 %reduce-scatter.30.cloned.1.call-start = ((), (), s32[]{:S(2)}) async-start(), calls=%async_computation.23 | async-start | bytes 589824 | tf_op jit(solution)/shard_map/reduce_scatter | solution.py:52
  760.1 262.7 %copy-start.9 = (bf16[72,8,4,384]{3,1,2,0:T(8,128)(2,1)S(1)}, bf16[72,8,4,384]{3,1,2,0:T(8,128)(2,1)}, u32[]{:S(2)}) copy-start(bf16[72,8,4,384]{3,1,2,0:T(8,128)(2,1)} %copy.351) | copy-start | bytes 5308420
  760.1 262.7 %copy-start.32 = (f32[64,576]{1,0:T(8,128)S(1)}, f32[64,576]{1,0:T(8,128)}, u32[]{:S(2)}) copy-start(f32[64,576]{1,0:T(8,128)} %copy-done.30) | copy-start | bytes 442372
  760.1 262.7 %copy-start.73 = (bf16[64,1536]{1,0:T(8,128)(2,1)S(1)}, bf16[64,1536]{1,0:T(8,128)(2,1)}, u32[]{:S(2)}) copy-start(bf16[64,1536]{1,0:T(8,128)(2,1)} %get-tuple-element.106) | copy-start | bytes 589828
  760.1 335.1 %all-reduce.10.cloned.1.call-start = ((), (), s32[]{:S(2)}) async-start(), calls=%async_computation.29 | async-start | bytes 3686400 | tf_op jit(solution)/shard_map/psum | solution.py:74
  1022.8 3.8 copy-start.123
  1023.5 4.0 copy-start.144
  1023.5 4.0 copy-start.145
  1023.5 4.0 copy-start.146
  1023.5 4.0 copy-start.147
  1023.5 52.3 %copy-start.107 = (f32[128,288]{1,0:T(8,128)S(1)}, f32[128,288]{1,0:T(8,128)}, u32[]{:S(2)}) copy-start(f32[128,288]{1,0:T(8,128)} %reduce-scatter.18.cloned.1.call-done) | copy-start | bytes 442372
  1023.5 52.3 %copy-start.108 = (f32[128,288]{1,0:T(8,128)S(1)}, f32[128,288]{1,0:T(8,128)}, u32[]{:S(2)}) copy-start(f32[128,288]{1,0:T(8,128)} %reduce-scatter.24.cloned.1.call-done) | copy-start | bytes 442372
  1095.2 4.5 copy-start.94
  (129 other events, 212.3 us)
Sparse Core Ops, SparseCore 0:
  11.1 25.6 all-gather.9
  38.4 37.2 all-gather.13
  77.9 45.0 all-gather.11
  407.3 32.0 reduce-scatter.13
  441.6 31.3 reduce-scatter.15
  484.6 6.5 reduce-scatter.17
  524.9 33.8 reduce-scatter.19
  561.0 31.2 reduce-scatter.21
  602.8 6.6 reduce-scatter.23
  634.3 32.8 reduce-scatter.27
  669.5 31.4 reduce-scatter.25
  703.2 41.9 reduce-scatter.33
  747.5 52.9 reduce-scatter.31
  802.7 75.0 reduce-scatter.37
  880.1 141.9 reduce-scatter.35
  1024.8 8.4 reduce-scatter.29
  1035.7 59.4 all-reduce.9
where the time goes:
time: 1120 us; the launch traced here: 1110 us
  waiting for transfers between devices  435 us (39%)
  blocking collectives  293 us (26%)
  local copies, waits for them, and re-layouts  217 us (19%)
  matrix products  79.1 us (7%)
  other arithmetic  56 us (5%)
  between operations  17.9 us (2%)
    reduce_scatter x10, waiting for transfers between devices, grid_sum(): lax.psum_scatter(items, ('row', 'col'), scatter_dimension=0, tiled=True)  408 us
    all_gather x7, blocking collectives, grid_gather(): lax.all_gather(for_sending(items), ('row', 'col'), axis=0, tiled=True)  196 us
    unnamed x2, blocking collectives  59.3 us
    unnamed x374, local copies, waits for them, and re-layouts  54.3 us
  transfers between devices with their start and end apart: 21, of which 13 were waited for; matrix products, arithmetic and copies ran while one was open for 14% of the time, Pallas kernels for 0%

commit v1 on v0

v1 whole, which is shorter than its diff:
```python
import functools

import jax
import jax.numpy as jnp
from jax import lax
from jax.experimental import pallas as pl
from jax.experimental.pallas import tpu as pltpu
from jax.sharding import PartitionSpec as P

HEADS = 9
KV_HEADS = 3
HEAD_DIM = 64
EPS = 1e-05
THETA = 100000.0
MESH = pl.DeviceIdType.MESH
F32 = jnp.float32
BF16 = jnp.bfloat16
VMEM_LIMIT = 56 * 1024 * 1024


def dot(left, right):
    return jnp.dot(left, right, preferred_element_type=F32)


def dot_tn(left, right):
    return lax.dot_general(left, right, (((0,), (0,)), ((), ())), preferred_element_type=F32)


def dot_nt(left, right):
    return lax.dot_general(left, right, (((1,), (1,)), ((), ())), preferred_element_type=F32)


def exchange(items, axis, collective_id):
    size = lax.axis_size(axis)
    count = len(items)

    def body(*refs):
        ins, outs = refs[:count], refs[count : 2 * count]
        send_sem, recv_sem, own_sem = refs[2 * count :]
        me = lax.axis_index(axis)
        barrier = pltpu.get_barrier_semaphore()
        for step in range(1, size):
            pl.semaphore_signal(
                barrier, inc=1, device_id={axis: lax.rem(me + step, size)}, device_id_type=MESH
            )
        pl.semaphore_wait(barrier, size - 1)

        def remote(no, step, target, slot):
            gather = items[no][1]
            return pltpu.make_async_remote_copy(
                src_ref=ins[no] if gather else ins[no].at[target],
                dst_ref=outs[no].at[slot],
                send_sem=send_sem.at[no, step - 1],
                recv_sem=recv_sem.at[no, step - 1],
                device_id={axis: target},
                device_id_type=MESH,
            )

        for step in range(1, size):
            for no in range(count):
                remote(no, step, lax.rem(me + step, size), me).start()
        local = [
            pltpu.make_async_copy(
                ins[no] if items[no][1] else ins[no].at[me], outs[no].at[me], own_sem.at[no]
            )
            for no in range(count)
        ]
        for copy in local:
            copy.start()
        for copy in local:
            copy.wait()
        for step in range(1, size):
            for no in range(count):
                source = lax.rem(me + size - step, size)
                remote(no, step, lax.rem(me + step, size), me).wait_send()
                remote(no, step, lax.rem(me + step, size), source).wait_recv()

    shapes = [
        jax.ShapeDtypeStruct((size,) + item.shape if gather else item.shape, item.dtype)
        for item, gather in items
    ]
    any_spec = pl.BlockSpec(memory_space=pl.ANY)
    return pl.pallas_call(
        body,
        out_shape=shapes,
        in_specs=[any_spec] * count,
        out_specs=[any_spec] * count,
        scratch_shapes=[
            pltpu.SemaphoreType.DMA((count, size - 1)),
            pltpu.SemaphoreType.DMA((count, size - 1)),
            pltpu.SemaphoreType.DMA((count,)),
        ],
        compiler_params=pltpu.CompilerParams(collective_id=collective_id, has_side_effects=True),
        name="exchange_%d" % collective_id,
    )(*[item for item, _ in items])


class Group:
    def __init__(self, rows_n, cols_n, send_sem, recv_sem):
        self.rows_n = rows_n
        self.size = rows_n * cols_n
        self.me = lax.axis_index("col") * rows_n + lax.axis_index("row")
        self.send_sem = send_sem
        self.recv_sem = recv_sem

    def peer(self, step):
        return lax.rem(self.me + step, self.size)

    def device(self, place):
        return {"col": place // self.rows_n, "row": lax.rem(place, self.rows_n)}

    def greet(self):
        barrier = pltpu.get_barrier_semaphore()
        for step in range(1, self.size):
            pl.semaphore_signal(
                barrier, inc=1, device_id=self.device(self.peer(step)), device_id_type=MESH
            )
        pl.semaphore_wait(barrier, self.size - 1)

    def block(self, ref, place, tokens):
        return ref.at[pl.ds(pl.multiple_of(place * tokens, tokens), tokens)]

    def copy(self, phase, step, src, dst):
        return pltpu.make_async_remote_copy(
            src_ref=src,
            dst_ref=dst,
            send_sem=self.send_sem.at[phase, step - 1],
            recv_sem=self.recv_sem.at[phase, step - 1],
            device_id=self.device(self.peer(step)),
            device_id_type=MESH,
        )

    def gather_start(self, phase, ref, tokens):
        own = self.block(ref, self.me, tokens)
        for step in range(1, self.size):
            self.copy(phase, step, own, own).start()

    def gather_wait(self, phase, ref, tokens):
        own = self.block(ref, self.me, tokens)
        for step in range(1, self.size):
            source = self.block(ref, self.peer(self.size - step), tokens)
            self.copy(phase, step, own, own).wait_send()
            self.copy(phase, step, own, source).wait_recv()

    def scatter_start(self, phase, ref, landing, tokens):
        for step in range(1, self.size):
            src = self.block(ref, self.peer(step), tokens)
            self.copy(phase, step, src, landing.at[step - 1]).start()

    def scatter_sum(self, phase, ref, landing, tokens):
        total = self.block(ref, self.me, tokens)[...].astype(F32)
        for step in range(1, self.size):
            src = self.block(ref, self.peer(step), tokens)
            copy = self.copy(phase, step, src, landing.at[step - 1])
            copy.wait_recv()
            total += landing[step - 1].astype(F32)
            copy.wait_send()
        return total


def turned(values):
    width = values.shape[1]
    lane = lax.broadcasted_iota(jnp.int32, values.shape, 1)
    first = lax.rem(lane, HEAD_DIM) < HEAD_DIM // 2
    ahead = pltpu.roll(values, width - HEAD_DIM // 2, 1)
    behind = pltpu.roll(values, HEAD_DIM // 2, 1)
    return jnp.where(first, -ahead, behind)


def three_heads(ref, base, group):
    start = base + group * 3 * HEAD_DIM
    return jnp.concatenate(
        [ref[:, start + h * HEAD_DIM : start + (h + 1) * HEAD_DIM] for h in range(3)], axis=0
    )


def probabilities(queries, keys, allowed):
    scores = dot_nt(queries, keys) * HEAD_DIM ** (-0.5)
    scores = jnp.where(allowed, scores, -1e30)
    raised = jnp.exp(scores - jnp.max(scores, axis=1, keepdims=True))
    return raised / jnp.sum(raised, axis=1, keepdims=True)


def allowed_pairs(own_seg, own_tok, all_seg):
    rows, length = own_seg.shape[0], all_seg.shape[1]
    spots = lax.broadcasted_iota(jnp.int32, (rows, length), 1)
    return (own_seg == all_seg) & (spots <= own_tok)


def forward_body(
    rows_n, cols_n,
    x_ref, gain_a, gain_f, wqkv, wout, wgu, wdn, cos, sin, own_seg, own_tok, all_seg,
    y_ref, a_ref, qkv_ref, kv_ref, o_ref, r_ref, b_ref, gu_ref, hid_ref,
    part, landing, send_sem, recv_sem,
):
    group = Group(rows_n, cols_n, send_sem, recv_sem)
    tokens, width = x_ref.shape
    kv_width = kv_ref.shape[1]
    ff = hid_ref.shape[1]
    group.greet()
    x = x_ref[...]
    scale = lax.rsqrt(jnp.mean(x * x, axis=1, keepdims=True) + EPS)
    a = (x * scale * gain_a[...]).astype(BF16)
    a_ref[...] = a
    raw = dot(a, wqkv[...]).astype(BF16).astype(F32)
    qkv_ref[...] = (raw * cos[...] + turned(raw) * sin[...]).astype(BF16)
    group.block(kv_ref, group.me, tokens)[...] = qkv_ref[:, :kv_width]
    group.gather_start(0, kv_ref, tokens)
    allowed = allowed_pairs(own_seg[...], own_tok[...], all_seg[...])
    group.gather_wait(0, kv_ref, tokens)
    half = kv_width // 2
    for g in range(KV_HEADS):
        keys = kv_ref[:, g * HEAD_DIM : (g + 1) * HEAD_DIM]
        values = kv_ref[:, half + g * HEAD_DIM : half + (g + 1) * HEAD_DIM]
        p = probabilities(three_heads(qkv_ref, kv_width, g), keys, allowed)
        out = dot(p.astype(BF16), values).astype(BF16)
        for h in range(3):
            at = (3 * g + h) * HEAD_DIM
            o_ref[:, at : at + HEAD_DIM] = out[h * tokens : (h + 1) * tokens]
    r = x + dot(o_ref[...], wout[...])
    r_ref[...] = r
    scale = lax.rsqrt(jnp.mean(r * r, axis=1, keepdims=True) + EPS)
    group.block(b_ref, group.me, tokens)[...] = (r * scale * gain_f[...]).astype(BF16)
    group.gather_start(1, b_ref, tokens)
    group.gather_wait(1, b_ref, tokens)
    gu_ref[...] = dot(b_ref[...], wgu[...])
    gate = gu_ref[:, :ff]
    hid_ref[...] = (gate / (1.0 + jnp.exp(-gate)) * gu_ref[:, ff:]).astype(BF16)
    part[...] = dot(hid_ref[...], wdn[...]).astype(BF16)
    group.scatter_start(2, part, landing, tokens)
    y_ref[...] = r_ref[...] + group.scatter_sum(2, part, landing, tokens)


def norm_back(x, gain, gz):
    scale = lax.rsqrt(jnp.mean(x * x, axis=1, keepdims=True) + EPS)
    weighted = gz * gain
    inner = jnp.mean(weighted * x, axis=1, keepdims=True)
    return (
        scale * weighted - x * (scale * scale * scale) * inner,
        jnp.sum(gz * x * scale, axis=0, keepdims=True),
    )


def backward_body(
    rows_n, cols_n,
    gy_ref, x_ref, gain_a, gain_f, wqkv, wout, wgu, wdn, cos, sin, own_seg, own_tok, all_seg,
    a_ref, qkv_ref, kv_ref, o_ref, r_ref, b_ref, gu_ref, hid_ref,
    gx_ref, gwqkv, gwout, gwgu, gwdn, ggain_a, ggain_f,
    gf_ref, ggu_ref, part, landing, kv_part, kv_landing, go_ref, gq_ref, gr_ref,
    send_sem, recv_sem,
):
    group = Group(rows_n, cols_n, send_sem, recv_sem)
    tokens, width = x_ref.shape
    kv_width = kv_ref.shape[1]
    half = kv_width // 2
    ff = hid_ref.shape[1]
    group.greet()
    group.block(gf_ref, group.me, tokens)[...] = gy_ref[...].astype(BF16)
    group.gather_start(0, gf_ref, tokens)
    group.gather_wait(0, gf_ref, tokens)
    ghid = dot_nt(gf_ref[...], wdn[...])
    gate = gu_ref[:, :ff]
    sig = 1.0 / (1.0 + jnp.exp(-gate))
    ggu_ref[:, :ff] = (ghid * gu_ref[:, ff:] * (sig * (1.0 + gate * (1.0 - sig)))).astype(BF16)
    ggu_ref[:, ff:] = (ghid * (gate * sig)).astype(BF16)
    part[...] = dot_nt(ggu_ref[...], wgu[...]).astype(BF16)
    group.scatter_start(1, part, landing, tokens)
    gwdn[...] = dot_tn(hid_ref[...], gf_ref[...]).astype(BF16)
    gwgu[...] = dot_tn(b_ref[...], ggu_ref[...]).astype(BF16)
    gb = group.scatter_sum(1, part, landing, tokens)
    grad, ggain_f[...] = norm_back(r_ref[...], gain_f[...], gb)
    gr = gy_ref[...] + grad
    gr_ref[...] = gr
    grad_b = gr.astype(BF16)
    go_ref[...] = dot_nt(grad_b, wout[...]).astype(BF16)
    allowed = allowed_pairs(own_seg[...], own_tok[...], all_seg[...])
    factor = HEAD_DIM ** (-0.5)
    gq_ref[...] = jnp.zeros_like(gq_ref)
    for g in range(KV_HEADS):
        keys = kv_ref[:, g * HEAD_DIM : (g + 1) * HEAD_DIM]
        values = kv_ref[:, half + g * HEAD_DIM : half + (g + 1) * HEAD_DIM]
        queries = three_heads(qkv_ref, kv_width, g)
        gout = three_heads(go_ref, 0, g)
        p = probabilities(queries, keys, allowed)
        gp = dot_nt(gout, values)
        gs = (p * (gp - jnp.sum(gp * p, axis=1, keepdims=True))).astype(BF16)
        gq = dot(gs, keys) * factor
        for h in range(3):
            at = kv_width + (3 * g + h) * HEAD_DIM
            gq_ref[:, at : at + HEAD_DIM] = gq[h * tokens : (h + 1) * tokens]
        at = g * HEAD_DIM
        kv_part[:, at : at + HEAD_DIM] = (dot_tn(gs, queries) * factor).astype(BF16)
        kv_part[:, half + at : half + at + HEAD_DIM] = dot_tn(p.astype(BF16), gout).astype(BF16)
    group.scatter_start(2, kv_part, kv_landing, tokens)
    gwout[...] = dot_tn(o_ref[...], gr_ref[...].astype(BF16)).astype(BF16)
    gq_ref[:, :kv_width] = group.scatter_sum(2, kv_part, kv_landing, tokens)
    g0 = gq_ref[...]
    packed = (g0 * cos[...] - turned(g0 * sin[...])).astype(BF16)
    ga = dot_nt(packed, wqkv[...])
    gwqkv[...] = dot_tn(a_ref[...], packed).astype(BF16)
    grad, ggain_a[...] = norm_back(x_ref[...], gain_a[...], ga)
    gx_ref[...] = gr_ref[...] + grad


def call_layer(body, operands, out_shapes, scratch, rows_n, cols_n, phases, collective_id, name):
    size = rows_n * cols_n
    spec = pl.BlockSpec(memory_space=pltpu.VMEM)
    return pl.pallas_call(
        functools.partial(body, rows_n, cols_n),
        out_shape=[jax.ShapeDtypeStruct(shape, kind) for shape, kind in out_shapes],
        in_specs=[spec] * len(operands),
        out_specs=[spec] * len(out_shapes),
        scratch_shapes=[pltpu.VMEM(shape, kind) for shape, kind in scratch]
        + [pltpu.SemaphoreType.DMA((phases, size - 1))] * 2,
        compiler_params=pltpu.CompilerParams(
            collective_id=collective_id, has_side_effects=True, vmem_limit_bytes=VMEM_LIMIT
        ),
        name=name,
    )(*operands)


def tables(segment_row, offset, row_count, kv_width, padded, used):
    own_ids = lax.dynamic_slice_in_dim(segment_row, offset, row_count)
    token_ids = offset + jnp.arange(row_count, dtype=jnp.int32)
    starts = jnp.sum((segment_row[None, :] < own_ids[:, None]).astype(jnp.int32), axis=1)
    positions = (token_ids - starts).astype(F32)
    frequency = THETA ** (-jnp.arange(HEAD_DIM // 2, dtype=F32) * 2.0 / HEAD_DIM)
    angles = positions[:, None] * frequency[None, :]
    lanes = jnp.arange(padded)
    turns = (lanes < kv_width // 2) | ((lanes >= kv_width) & (lanes < used))
    repeat = padded // (HEAD_DIM // 2)
    cos = jnp.where(turns[None, :], jnp.tile(jnp.cos(angles), (1, repeat)), 1.0)
    sin = jnp.where(turns[None, :], jnp.tile(jnp.sin(angles), (1, repeat)), 0.0)
    return cos, sin, jnp.tile(own_ids, 3)[:, None], jnp.tile(token_ids, 3)[:, None]


def on_device(
    inputs, segments, cotangent, gain_attn, w_query, w_key, w_value, w_out, gain_ffn,
    w_gate, w_up, w_down,
):
    rows_n, cols_n = lax.axis_size("row"), lax.axis_size("col")
    section = lax.axis_index("section")
    size = rows_n * cols_n
    length = segments.shape[2]
    tokens = length // size
    band = w_query.shape[1]
    width = band * rows_n
    qc, kc = w_query.shape[2], w_key.shape[2]
    kv_width = 2 * kc * cols_n
    used = kv_width + qc * cols_n
    padded = -(-used // 128) * 128
    fc = w_gate.shape[2] // rows_n
    fp = -(-fc // 128) * 128

    qkv = jnp.concatenate([w_key[0], w_value[0], w_query[0]], axis=1)
    gate_up = jnp.stack(
        [w_gate[0].reshape(band, rows_n, fc), w_up[0].reshape(band, rows_n, fc)], axis=2
    ).transpose(1, 0, 2, 3).reshape(rows_n, band, 2 * fc)
    down = w_down[0].reshape(rows_n, fc, band)
    gains = jnp.stack([gain_attn[0], gain_ffn[0]])
    qkv, out, gate_up, down, gains = exchange(
        [(qkv, True), (w_out[0], True), (gate_up, True), (down, True), (gains, True)], "section", 0
    )
    qkv, out = exchange([(qkv, True), (out, True)], "col", 1)
    mine = lax.dynamic_index_in_dim(inputs[0], section, 0, False).reshape(rows_n, tokens, band)
    cot = lax.dynamic_index_in_dim(cotangent[0], section, 0, False).reshape(rows_n, tokens, band)
    qkv, out, gate_up, down, gains, mine, cot = exchange(
        [
            (qkv, True), (out, True),
            (gate_up.transpose(1, 0, 2, 3), False), (down.transpose(1, 0, 2, 3), False),
            (gains, True), (mine, False), (cot, False),
        ],
        "row", 2,
    )
    layers = gains.shape[1]
    pad = jnp.zeros((width, padded - used), BF16)
    full = []
    for n in range(layers):
        part = qkv[:, :, n].transpose(0, 2, 1, 3)
        part = jnp.concatenate(
            [
                part[..., :kc].reshape(width, -1),
                part[..., kc : 2 * kc].reshape(width, -1),
                part[..., 2 * kc :].reshape(width, -1),
                pad,
            ],
            axis=1,
        )
        wout = out[:, :, n].transpose(1, 2, 0, 3).reshape(width, width)
        wgu = jnp.pad(
            gate_up[:, n].reshape(width, 2, fc), ((0, 0), (0, 0), (0, fp - fc))
        ).reshape(width, 2 * fp)
        wdn = jnp.pad(
            down[:, n].transpose(1, 0, 2).reshape(fc, width), ((0, fp - fc), (0, 0))
        )
        gain = gains[:, n].transpose(1, 0, 2).reshape(2, 1, width).astype(F32)
        full.append((gain[0], gain[1], part, wout, wgu, wdn))

    segment_row = lax.dynamic_index_in_dim(segments[0], section, 0, False)
    place = lax.axis_index("col") * rows_n + lax.axis_index("row")
    cos, sin, own_seg, own_tok = tables(
        segment_row, place * tokens, tokens, kv_width, padded, used
    )
    table_set = (cos, sin, own_seg, own_tok, segment_row[None, :])

    entry = mine.transpose(1, 0, 2).reshape(tokens, width).astype(F32)
    saved, acts = [], []
    for n in range(layers):
        y, *kept = call_layer(
            forward_body,
            (entry, *full[n], *table_set),
            [
                ((tokens, width), F32), ((tokens, width), BF16), ((tokens, padded), BF16),
                ((length, kv_width), BF16), ((tokens, width), BF16), ((tokens, width), F32),
                ((length, width), BF16), ((length, 2 * fp), F32), ((length, fp), BF16),
            ],
            [((length, width), BF16), ((size - 1, tokens, width), BF16)],
            rows_n, cols_n, 3, 3, "layer_forward",
        )
        saved.append((entry, kept))
        acts.append(y.astype(BF16))
        entry = acts[-1].astype(F32)

    grad = cot.transpose(1, 0, 2).reshape(tokens, width).astype(F32)
    grads, weight_grads = [None] * layers, [None] * layers
    for n in reversed(range(layers)):
        entry, kept = saved[n]
        grads[n], *weight_grads[n] = call_layer(
            backward_body,
            (grad, entry, *full[n], *table_set, *kept),
            [
                ((tokens, width), F32), ((width, padded), BF16), ((width, width), BF16),
                ((width, 2 * fp), BF16), ((fp, width), BF16), ((1, width), F32), ((1, width), F32),
            ],
            [
                ((length, width), BF16), ((length, 2 * fp), BF16), ((length, width), BF16),
                ((size - 1, tokens, width), BF16), ((length, kv_width), BF16),
                ((size - 1, tokens, kv_width), BF16), ((tokens, width), BF16),
                ((tokens, padded), F32), ((tokens, width), F32),
            ],
            rows_n, cols_n, 3, 4, "layer_backward",
        )
        grad = grads[n].astype(BF16).astype(F32)

    def qkv_blocks(item):
        key, value, query = (
            item[:, at : at + cols_n * cut].reshape(rows_n, band, cols_n, cut)
            for at, cut in ((0, kc), (kv_width // 2, kc), (kv_width, qc))
        )
        return jnp.concatenate([key, value, query], axis=3).transpose(0, 2, 1, 3)

    g_qkv = jnp.stack([qkv_blocks(item[0]) for item in weight_grads], axis=1)
    out_rows = width // cols_n
    g_out = jnp.stack(
        [
            item[1].reshape(cols_n, out_rows, rows_n, band).transpose(2, 0, 1, 3)
            for item in weight_grads
        ],
        axis=1,
    )
    g_gu = jnp.stack(
        [
            item[2].reshape(rows_n, band, 2, fp)[..., :fc].reshape(rows_n, band, 2 * fc)
            for item in weight_grads
        ],
        axis=1,
    )
    g_dn = jnp.stack(
        [item[3][:fc].reshape(fc, rows_n, band).transpose(1, 0, 2) for item in weight_grads],
        axis=1,
    )
    g_gain = jnp.stack(
        [jnp.stack([item[4], item[5]]).reshape(2, rows_n, band) for item in weight_grads]
    ).transpose(2, 0, 1, 3)
    act = jnp.stack(acts).reshape(layers, tokens, rows_n, band).transpose(2, 0, 1, 3)
    in_grad = jnp.stack(grads).reshape(layers, tokens, rows_n, band).transpose(2, 0, 1, 3)
    g_qkv, g_out, g_gu, g_dn, g_gain, act, in_grad = exchange(
        [(item, False) for item in (g_qkv, g_out, g_gu, g_dn, g_gain, act, in_grad)], "row", 5
    )

    def add(item):
        return jnp.sum(item.astype(F32), axis=0)

    g_qkv, g_out, g_gu, g_dn, g_gain, act, in_grad = exchange(
        [
            (add(g_qkv).astype(BF16), False), (add(g_out).astype(BF16), False),
            (g_gu.transpose(1, 0, 2, 3), False), (g_dn.transpose(1, 0, 2, 3), False),
            (add(g_gain), False),
            (act.transpose(1, 0, 2, 3), False), (in_grad.transpose(1, 0, 2, 3), False),
        ],
        "section", 6,
    )
    activations = act.reshape((1, 1) + inputs.shape[1:])
    input_grads = in_grad.reshape((1, 1) + inputs.shape[1:])
    g_qkv, g_out, g_gain = exchange(
        [(add(g_qkv).astype(BF16), False), (add(g_out).astype(BF16), False), (add(g_gain), True)],
        "col", 7,
    )
    g_qkv, g_out, g_gu, g_dn, g_gain = (
        add(item)
        for item in exchange(
            [
                (add(g_qkv).astype(BF16), True), (add(g_out).astype(BF16), True),
                (add(g_gu).astype(BF16), True), (add(g_dn).astype(BF16), True),
                (add(g_gain), True),
            ],
            "dp", 8,
        )
    )
    g_gu = g_gu.reshape(rows_n, band, 2, fc).transpose(2, 1, 0, 3).reshape(2, band, rows_n * fc)
    return (
        activations, input_grads, g_gain[0][None], g_qkv[:, 2 * kc :][None], g_qkv[:, :kc][None],
        g_qkv[:, kc : 2 * kc][None], g_out[None], g_gain[1][None], g_gu[0][None], g_gu[1][None],
        g_dn.reshape(rows_n * fc, band)[None],
    )


def solution(mesh):
    grid = P("section", "row", "col")
    turned_grid = P("section", "col", "row")
    gain = P("section", "row")
    tokens = P("dp", None, "col", "row")
    result = P("section", "dp", None, "col", "row")
    weights = (gain, grid, grid, grid, turned_grid, gain, grid, grid, turned_grid)
    return jax.shard_map(
        on_device,
        mesh=mesh,
        in_specs=(tokens, P("dp", None, None), tokens) + weights,
        out_specs=(result, result) + weights,
        check_vma=False,
    )
```

time: 1120 us -> 707 us (0.63)
  Pallas kernels: 0 us -> 583 us
  waiting for transfers between devices: 435 us -> 0 us
  blocking collectives: 293 us -> 0 us
  local copies, waits for them, and re-layouts: 217 us -> 70.5 us
  matrix products: 79.1 us -> 0 us
  other arithmetic: 56 us -> 39.4 us
  between operations: 17.9 us -> 2.2 us
    pallas_call x0 -> x11, Pallas kernels: none -> 583 us  [the longest x7 379 us: exchange(): pl.pallas_call(body, out_shape=shapes, in_specs=[any_spec] * count, out_s...]
    reduce_scatter x13 -> x0, waiting for transfers between devices: 412 us -> none  [the longest x10 408 us: grid_sum(): lax.psum_scatter(items, ('row', 'col'), scatter_dimension=0, tiled=True)]
    all_gather x16 -> x0, blocking collectives: 215 us -> none  [the longest x7 196 us: grid_gather(): lax.all_gather(for_sending(items), ('row', 'col'), axis=0, tiled=True)]
    dot_general x57 -> x0, matrix products: 79.1 us -> none  [the longest x12 21.1 us: matmul_nt(): lax.dot_general(left, right, (((1,), (1,)), ((), ())), preferred_element_...]
    unnamed x2 -> x0, blocking collectives: 59.3 us -> none
    reshape x31 -> x40, local copies, waits for them, and re-layouts: 67.1 us -> 21.4 us  [the longest x12 4.4 us: qkv_blocks(): item[:, at:at + cols_n * cut].reshape(rows_n, band, cols_n, cut)]
    unnamed x374 -> x112, local copies, waits for them, and re-layouts: 54.3 us -> 12.3 us
    transpose x21 -> x7, local copies, waits for them, and re-layouts: 38.7 us -> 4.46 us  [the longest x3 2 us: on_device(): wout = out[:, :, n].transpose(1, 2, 0, 3).reshape(width, width)]
  transfers between devices with their start and end apart: 21 -> 0, of which waited for: 13 -> 0; matrix products, arithmetic and copies ran while one was open for 14% -> 0% of each run, Pallas kernels for 0% -> 0%
where the time goes in v1:
time: 707 us; the launch traced here: 695 us
  Pallas kernels  583 us (82%)
  local copies, waits for them, and re-layouts  70.5 us (10%)
  other arithmetic  39.4 us (6%)
    pallas_call x7, Pallas kernels, exchange(): pl.pallas_call(body, out_shape=shapes, in_specs=[any_spec] * count, out_s...  379 us
    pallas_call x4, Pallas kernels, call_layer(): pl.pallas_call(functools.partial(body, rows_n, cols_n), out_shape=[jax.Sh...  204 us
    reduce_sum x16, other arithmetic, add(): return jnp.sum(item.astype(F32), axis=0)  18.5 us

profile of v1, /device:TPU:0, one launch (start us, length us, event | category | flops | bytes accessed | tf_op | source)
XLA Modules:
  0.0 694.7 jit_solution(13064872761571318105)
XLA Ops:
  0.7 1.0 constant_dynamic-slice_fusion.2
  3.2 1.1 stack_reshape_squeeze.6
  5.5 1.5 maximum_bitcast_fusion.2
  7.0 1.1 reshape.280.refs_2_
  9.3 0.9 copy.256
  10.7 34.4 %exchange_0.1 = (bf16[2,288,240]{2,1,0:T(8,128)(2,1)}, bf16[2,144,288]{2,1,0:T(8,128)(2,1)}, bf16[2,2,288,384]{3,2,1,0:T(8,128)(2,1)}, bf16[2,2,192,288]{3,2,1,0:T(8,128)(2,1)}, bf16[2,2,288]{2,1,0:T(2,128)(2,1)}) custom-call(bf16[288,240]{1,0:T(8,128)(2,1)} %pad_maximum_fusion.4.refs_0_, bf16[144,288]{1,0:T(8,128)(2,1)} %bitcast.158, ...), custom_call_target="tpu_custom_call" | custom-call | tf_op jit(solution)/shard_map/exchange_0/pallas_call | solution.py:83
  45.1 38.0 %exchange_1.1 = (bf16[4,2,288,240]{3,2,1,0:T(8,128)(2,1)}, bf16[4,2,144,288]{3,2,1,0:T(8,128)(2,1)}) custom-call(bf16[2,288,240]{2,1,0:T(8,128)(2,1)} %get-tuple-element.79.refs_0_, bf16[2,144,288]{2,1,0:T(8,128)(2,1)} %get-tuple-element.80.refs_1_), custom_call_target="tpu_custom_call" | custom-call | tf_op jit(solution)/shard_map/exchange_1/pallas_call | solution.py:83
  83.1 2.2 copy.360
  85.3 0.9 copy.362
  86.2 89.3 %exchange_2.1 = (bf16[2,4,2,288,240]{4,3,2,1,0:T(8,128)(2,1)}, bf16[2,4,2,144,288]{4,3,2,1,0:T(8,128)(2,1)}, bf16[2,2,288,384]{3,2,1,0:T(8,128)(2,1)}, bf16[2,2,...) custom-call(bf16[4,2,288,240]{3,2,1,0:T(8,128)(2,1)} %get-tuple-elem, ...), custom_call_target="tpu_custom_call" | custom-call | tf_op jit(solution)/shard_map/exchange_2/pallas_call | solution.py:83
  175.4 1.8 slice_bitcast_fusion
  177.8 1.0 reshape.314
  179.2 1.0 reshape.315
  180.8 1.0 reshape.317
  182.2 1.0 reshape.318
  183.7 0.9 copy.323
  185.9 0.9 copy.326
  187.9 3.6 maximum_maximum_fusion.1
  194.9 0.9 copy.269
  195.8 1.5 reshape.286.wout
  198.3 0.9 copy.345
  203.8 52.8 %layer_forward.2 = (f32[64,576]{1,0:T(8,128)}, bf16[64,576]{1,0:T(8,128)(2,1)}, bf16[64,1024]{1,0:T(8,128)(2,1)}, bf16[512,384]{1,0:T(8,128)(2,1)}, bf16[64,576]...) custom-call(f32[64,576]{1,0:T(8,128)} %reshape.311.x_ref, ...), custom_call_target="tpu_custom_call" | custom-call | tf_op jit(solution)/shard_map/layer_forward/pallas_call | solution.py:308
  256.6 1.6 fusion.3
  259.6 0.9 copy.281
  260.5 1.5 reshape.292.wout
  262.9 1.0 copy.346
  265.1 48.1 %layer_forward.3 = (f32[64,576]{1,0:T(8,128)}, bf16[64,576]{1,0:T(8,128)(2,1)}, bf16[64,1024]{1,0:T(8,128)(2,1)}, bf16[512,384]{1,0:T(8,128)(2,1)}, bf16[64,576]...) custom-call(f32[64,576]{1,0:T(8,128)} %get-tuple-element.206.x_ref, ...), custom_call_target="tpu_custom_call" | custom-call | tf_op jit(solution)/shard_map/layer_forward/pallas_call | solution.py:308
  314.3 53.1 %layer_backward.2 = (f32[64,576]{1,0:T(8,128)}, bf16[576,1024]{1,0:T(8,128)(2,1)}, bf16[576,576]{1,0:T(8,128)(2,1)}, bf16[576,512]{1,0:T(8,128)(2,1)}, bf16[256,...) custom-call(f32[64,576]{1,0:T(8,128)} %reshape.310.gy_ref, f32[64,576]{1,0:T(8,128)} %get-tuple-element.206.x_ref, ...), custom_call_target="tpu_custom_call" | custom-call | tf_op jit(solution)/shard_map/layer_backward/pallas_call | solution.py:308
  367.4 1.6 convert_convert_fusion.gy_ref
  369.0 50.0 %layer_backward.3 = (f32[64,576]{1,0:T(8,128)}, bf16[576,1024]{1,0:T(8,128)(2,1)}, bf16[576,576]{1,0:T(8,128)(2,1)}, bf16[576,512]{1,0:T(8,128)(2,1)}, bf16[256,...) custom-call(f32[64,576]{1,0:T(8,128)} %convert_convert_fusion.gy_ref, f32[64,576]{1,0:T(8,128)} %reshape.311.x_ref, ...), custom_call_target="tpu_custom_call" | custom-call | tf_op jit(solution)/shard_map/layer_backward/pallas_call | solution.py:308
  419.0 1.1 stack.97
  424.1 0.9 pad_maximum_fusion.3.refs_3_
  426.5 1.0 pad_maximum_fusion.2.refs_2_
  427.5 0.8 reshape.301
  428.5 1.0 copy-done.13
  429.5 0.8 reshape.302
  430.5 1.5 pad_maximum_fusion.1.refs_1_
  434.1 1.1 maximum_bitcast_fusion
  436.4 1.1 copy-done.5
  437.5 0.9 fusion.6
  438.7 1.3 reshape.324
  440.1 1.1 maximum_bitcast_fusion.1
  441.2 2.1 pad_maximum_fusion.refs_0_
  443.3 96.4 %exchange_5.1 = (bf16[2,2,4,288,240]{4,3,2,1,0:T(8,128)(2,1)}, bf16[2,2,4,144,288]{4,3,2,1,0:T(8,128)(2,1)}, bf16[2,2,288,384]{3,2,1,0:T(8,128)(2,1)}, bf16[2,2,...) custom-call(bf16[2,2,4,288,240]{4,3,2,1,0:T(8,128)(2,1)} %pad_maximu, ...), custom_call_target="tpu_custom_call" | custom-call | tf_op jit(solution)/shard_map/exchange_5/pallas_call | solution.py:83
  539.8 3.6 reduce_sum.178.refs_0_
  543.4 1.0 copy.357
  545.2 1.6 reduce_sum.179.refs_1_
  546.8 0.9 copy.361
  549.9 64.5 %exchange_6.1 = (bf16[2,4,288,240]{3,2,1,0:T(8,128)(2,1)}, bf16[2,4,144,288]{3,2,1,0:T(8,128)(2,1)}, bf16[2,2,288,384]{3,2,1,0:T(8,128)(2,1)}, bf16[2,2,192,288]...) custom-call(bf16[2,4,288,240]{3,2,1,0:T(8,128)(2,1)} %reduce_sum.178.refs_0, ...), custom_call_target="tpu_custom_call" | custom-call | tf_op jit(solution)/shard_map/exchange_6/pallas_call | solution.py:83
  614.4 2.6 reduce_sum.181.refs_0_
  617.0 1.1 reduce_sum.182.refs_1_
  618.7 23.0 %exchange_7.1 = (bf16[4,288,240]{2,1,0:T(8,128)(2,1)}, bf16[4,144,288]{2,1,0:T(8,128)(2,1)}, f32[4,2,288]{2,1,0:T(2,128)}) custom-call(bf16[4,288,240]{2,1,0:T(8,128)(2,1)} %reduce_sum.181.refs_0_, bf16[4,144,288]{2,1,0:T(8,128)(2,1)} %reduce_sum.182.refs_1_, f32[2,288]{1,0:T(2,128)} %reduce_sum.183.refs_2_), custom_call_target="tpu_custom_call" | custom-call | tf_op jit(solution)/shard_map/exchange_7/pallas_call | solution.py:83
  641.6 1.9 reduce_sum.184.refs_0_
  643.6 1.8 reduce_sum.185.refs_1_
  645.9 1.0 reduce_sum.186.refs_2_
  647.0 0.9 reduce_sum.187.refs_3_
  647.9 33.0 %exchange_8.1 = (bf16[2,288,240]{2,1,0:T(8,128)(2,1)}, bf16[2,144,288]{2,1,0:T(8,128)(2,1)}, bf16[2,2,288,384]{3,2,1,0:T(8,128)(2,1)}, bf16[2,2,192,288]{3,2,1,0:T(8,128)(2,1)}, f32[2,2,288]{2,1,0:T(2,128)}) custom-call(bf16[288,240]{1,0:T(8,128)(2,1)} %reduce_sum.184.refs_0_, bf16[144,288]{1,0:T(8,128)(2,1)} %reduce_sum.185.refs_1_, ...), custom_call_target="tpu_custom_call" | custom-call | tf_op jit(solution)/shard_map/exchange_8/pallas_call | solution.py:83
  680.9 1.4 convert_reduce_fusion
  682.3 0.8 reshape.309
  683.2 0.9 fusion.4
  684.6 1.2 slice.157
  686.3 1.2 slice.159
  687.6 1.0 copy.320
  692.5 0.9 copy.316
  (226 shorter events, 41.3 us)
Async XLA Ops:
  0.6 190.9 %copy-start = (s32[1,2,512]{2,1,0:T(2,128)S(1)}, s32[1,2,512]{2,1,0:T(2,128)}, u32[]{:S(2)}) copy-start(s32[1,2,512]{2,1,0:T(2,128)} %param.13) | copy-start | bytes 12292
  0.7 4.1 copy-start.27
  5.4 2.6 copy-start.34
  5.4 2.7 copy-start.37
  5.5 2.8 copy-start.38
  6.9 2.3 copy-start.28
  6.9 3.2 copy-start.48
  7.0 3.2 copy-start.49
  45.1 40.2 %copy-start.22 = (bf16[2,2,192,288]{3,2,1,0:T(8,128)(2,1)S(1)}, bf16[2,2,192,288]{3,2,1,0:T(8,128)(2,1)}, u32[]{:S(2)}) copy-start(bf16[2,2,192,288]{3,2,1,0:T(8,128)(2,1)} %get-tuple-element.84) | copy-start | bytes 1327108
  186.8 1.0 copy-start.7
  186.8 1.0 copy-start.8
  192.2 1.1 copy-start.43
  192.2 2.5 copy-start.2
  195.8 1.6 copy-start.9
  197.8 1.5 copy-start.16
  199.2 1.4 copy-start.36
  265.1 48.1 %copy-start.35 = (bf16[2,64,288]{2,1,0:T(8,128)(2,1)S(1)}, bf16[2,64,288]{2,1,0:T(8,128)(2,1)}, u32[]{:S(2)}) copy-start(bf16[2,64,288]{2,1,0:T(8,128)(2,1)} %get-tuple-element.86) | copy-start | bytes 221188
  369.0 51.1 %copy-start.15 = (f32[64,576]{1,0:T(8,128)S(1)}, f32[64,576]{1,0:T(8,128)}, u32[]{:S(2)}) copy-start(f32[64,576]{1,0:T(8,128)} %get-tuple-element.102) | copy-start | bytes 442372
  419.0 2.2 copy-start.33
  420.4 1.9 copy-start.47
  420.4 2.0 copy-start.46
  420.4 2.1 copy-start.45
  420.4 2.2 copy-start.44
  420.4 2.9 copy-start.32
  421.5 2.1 copy-start.31
  423.7 1.3 copy-start.18
  425.0 1.1 copy-start.17
  426.2 1.3 copy-start.14
  428.4 1.1 copy-start.13
  430.5 1.6 copy-start.6
  434.0 1.3 copy-start.4
  436.2 1.3 copy-start.5
  539.8 3.6 copy-start.11
  543.4 1.8 copy-start.3
  545.2 1.6 copy-start.21
  546.8 1.1 copy-start.23
  546.8 1.8 copy-start.29
  546.8 2.5 copy-start.39
  614.4 2.6 copy-start.12
  614.4 3.7 copy-start.42
  618.1 27.9 %copy-start.10 = (bf16[2,2,288,384]{3,2,1,0:T(8,128)(2,1)S(1)}, bf16[2,2,288,384]{3,2,1,0:T(8,128)(2,1)}, u32[]{:S(2)}) copy-start(bf16[2,2,288,384]{3,2,1,0:T(8,128)(2,1)} %get-tuple-element.139) | copy-start | bytes 2654212
  641.6 3.7 copy-start.40
  641.6 5.3 copy-start.19
  685.8 1.7 copy-start.20
  687.5 1.1 copy-start.25
  688.6 2.6 copy-start.26
  688.6 3.3 copy-start.41
  688.6 3.9 copy-start.24
  688.8 5.4 copy-start.1
  689.6 3.8 copy-start.30

commit v2 on v1

--- a/solution.py
+++ b/solution.py
@@ -30,23 +30,30 @@
     return lax.dot_general(left, right, (((1,), (1,)), ((), ())), preferred_element_type=F32)
 
 
-def exchange(items, axis, collective_id):
-    size = lax.axis_size(axis)
+def exchange(items, collective_id):
     count = len(items)
+    axes = sorted({axis for _, axis, _ in items})
+    most = max(lax.axis_size(axis) for axis in axes) - 1
 
     def body(*refs):
         ins, outs = refs[:count], refs[count : 2 * count]
         send_sem, recv_sem, own_sem = refs[2 * count :]
-        me = lax.axis_index(axis)
         barrier = pltpu.get_barrier_semaphore()
-        for step in range(1, size):
-            pl.semaphore_signal(
-                barrier, inc=1, device_id={axis: lax.rem(me + step, size)}, device_id_type=MESH
-            )
-        pl.semaphore_wait(barrier, size - 1)
-
-        def remote(no, step, target, slot):
-            gather = items[no][1]
+
+        def other(axis, step):
+            size = lax.axis_size(axis)
+            return lax.rem(lax.axis_index(axis) + step + size, size)
+
+        for axis in axes:
+            for step in range(1, lax.axis_size(axis)):
+                pl.semaphore_signal(
+                    barrier, inc=1, device_id={axis: other(axis, step)}, device_id_type=MESH
+                )
+        pl.semaphore_wait(barrier, sum(lax.axis_size(axis) - 1 for axis in axes))
+
+        def remote(no, step, slot):
+            _, axis, gather = items[no]
+            target = other(axis, step)
             return pltpu.make_async_remote_copy(
                 src_ref=ins[no] if gather else ins[no].at[target],
                 dst_ref=outs[no].at[slot],
@@ -56,105 +63,140 @@
                 device_id_type=MESH,
             )
 
-        for step in range(1, size):
-            for no in range(count):
-                remote(no, step, lax.rem(me + step, size), me).start()
-        local = [
-            pltpu.make_async_copy(
-                ins[no] if items[no][1] else ins[no].at[me], outs[no].at[me], own_sem.at[no]
-            )
-            for no in range(count)
-        ]
+        for no, (_, axis, gather) in enumerate(items):
+            for step in range(1, lax.axis_size(axis)):
+                remote(no, step, lax.axis_index(axis)).start()
+        local = []
+        for no, (_, axis, gather) in enumerate(items):
+            me = lax.axis_index(axis)
+            src = ins[no] if gather else ins[no].at[me]
+            local.append(pltpu.make_async_copy(src, outs[no].at[me], own_sem.at[no]))
         for copy in local:
             copy.start()
         for copy in local:
             copy.wait()
-        for step in range(1, size):
-            for no in range(count):
-                source = lax.rem(me + size - step, size)
-                remote(no, step, lax.rem(me + step, size), me).wait_send()
-                remote(no, step, lax.rem(me + step, size), source).wait_recv()
+        for no, (_, axis, gather) in enumerate(items):
+            for step in range(1, lax.axis_size(axis)):
+                remote(no, step, lax.axis_index(axis)).wait_send()
+                remote(no, step, other(axis, -step)).wait_recv()
 
     shapes = [
-        jax.ShapeDtypeStruct((size,) + item.shape if gather else item.shape, item.dtype)
-        for item, gather in items
+        jax.ShapeDtypeStruct(
+            (lax.axis_size(axis),) + item.shape if gather else item.shape, item.dtype
+        )
+        for item, axis, gather in items
     ]
-    any_spec = pl.BlockSpec(memory_space=pl.ANY)
+    spec = pl.BlockSpec(memory_space=pltpu.VMEM)
     return pl.pallas_call(
         body,
         out_shape=shapes,
-        in_specs=[any_spec] * count,
-        out_specs=[any_spec] * count,
+        in_specs=[spec] * count,
+        out_specs=[spec] * count,
         scratch_shapes=[
-            pltpu.SemaphoreType.DMA((count, size - 1)),
-            pltpu.SemaphoreType.DMA((count, size - 1)),
+            pltpu.SemaphoreType.DMA((count, most)),
+            pltpu.SemaphoreType.DMA((count, most)),
             pltpu.SemaphoreType.DMA((count,)),
         ],
-        compiler_params=pltpu.CompilerParams(collective_id=collective_id, has_side_effects=True),
+        compiler_params=pltpu.CompilerParams(
+            collective_id=collective_id, has_side_effects=True, vmem_limit_bytes=VMEM_LIMIT
+        ),
         name="exchange_%d" % collective_id,
-    )(*[item for item, _ in items])
+    )(*[item for item, _, _ in items])
 
 
 class Group:
-    def __init__(self, rows_n, cols_n, send_sem, recv_sem):
-        self.rows_n = rows_n
-        self.size = rows_n * cols_n
-        self.me = lax.axis_index("col") * rows_n + lax.axis_index("row")
-        self.send_sem = send_sem
-        self.recv_sem = recv_sem
-
-    def peer(self, step):
-        return lax.rem(self.me + step, self.size)
-
-    def device(self, place):
-        return {"col": place // self.rows_n, "row": lax.rem(place, self.rows_n)}
+    def __init__(self, rows_n, cols_n, far_send, far_recv, near_send, near_recv):
+        self.rows_n, self.cols_n = rows_n, cols_n
+        self.row, self.col = lax.axis_index("row"), lax.axis_index("col")
+        self.me = self.place(0, self.row)
+        self.far_send, self.far_recv = far_send, far_recv
+        self.near_send, self.near_recv = near_send, near_recv
+
+    def place(self, step, row):
+        return lax.rem(self.col + step + self.cols_n, self.cols_n) * self.rows_n + row
 
     def greet(self):
         barrier = pltpu.get_barrier_semaphore()
-        for step in range(1, self.size):
+        for step in range(1, self.cols_n):
             pl.semaphore_signal(
-                barrier, inc=1, device_id=self.device(self.peer(step)), device_id_type=MESH
+                barrier,
+                inc=1,
+                device_id={"col": lax.rem(self.col + step, self.cols_n)},
+                device_id_type=MESH,
             )
-        pl.semaphore_wait(barrier, self.size - 1)
+        pl.semaphore_signal(barrier, inc=1, device_id={"row": 1 - self.row}, device_id_type=MESH)
+        pl.semaphore_wait(barrier, self.cols_n)
 
     def block(self, ref, place, tokens):
         return ref.at[pl.ds(pl.multiple_of(place * tokens, tokens), tokens)]
 
-    def copy(self, phase, step, src, dst):
+    def far(self, phase, step, src, dst):
         return pltpu.make_async_remote_copy(
             src_ref=src,
             dst_ref=dst,
-            send_sem=self.send_sem.at[phase, step - 1],
-            recv_sem=self.recv_sem.at[phase, step - 1],
-            device_id=self.device(self.peer(step)),
+            send_sem=self.far_send.at[phase, step - 1],
+            recv_sem=self.far_recv.at[phase, step - 1],
+            device_id={"col": lax.rem(self.col + step, self.cols_n)},
+            device_id_type=MESH,
+        )
+
+    def near(self, phase, step, src, dst):
+        return pltpu.make_async_remote_copy(
+            src_ref=src,
+            dst_ref=dst,
+            send_sem=self.near_send.at[phase, step],
+            recv_sem=self.near_recv.at[phase, step],
+            device_id={"row": 1 - self.row},
             device_id_type=MESH,
         )
 
     def gather_start(self, phase, ref, tokens):
         own = self.block(ref, self.me, tokens)
-        for step in range(1, self.size):
-            self.copy(phase, step, own, own).start()
+        for step in range(1, self.cols_n):
+            self.far(phase, step, own, own).start()
+        self.near(phase, 0, own, own).start()
 
     def gather_wait(self, phase, ref, tokens):
         own = self.block(ref, self.me, tokens)
-        for step in range(1, self.size):
-            source = self.block(ref, self.peer(self.size - step), tokens)
-            self.copy(phase, step, own, own).wait_send()
-            self.copy(phase, step, own, source).wait_recv()
-
-    def scatter_start(self, phase, ref, landing, tokens):
-        for step in range(1, self.size):
-            src = self.block(ref, self.peer(step), tokens)
-            self.copy(phase, step, src, landing.at[step - 1]).start()
-
-    def scatter_sum(self, phase, ref, landing, tokens):
-        total = self.block(ref, self.me, tokens)[...].astype(F32)
-        for step in range(1, self.size):
-            src = self.block(ref, self.peer(step), tokens)
-            copy = self.copy(phase, step, src, landing.at[step - 1])
-            copy.wait_recv()
+        for step in range(1, self.cols_n):
+            came = self.block(ref, self.place(-step, self.row), tokens)
+            self.far(phase, step, own, came).wait_recv()
+            self.near(phase, step, came, came).start()
+        for step in range(self.cols_n):
+            came = self.block(ref, self.place(-step, self.row), tokens)
+            relayed = self.block(ref, self.place(-step, 1 - self.row), tokens)
+            self.near(phase, step, came, came).wait_send()
+            self.near(phase, step, came, relayed).wait_recv()
+        for step in range(1, self.cols_n):
+            self.far(phase, step, own, own).wait_send()
+
+    def scatter_near(self, phase, ref, pair, tokens):
+        for step in [*range(1, self.cols_n), 0]:
+            src = self.block(ref, self.place(step, 1 - self.row), tokens)
+            self.near(phase, step, src, pair.at[step]).start()
+
+    def scatter_far(self, phase, ref, pair, landing, tokens):
+        for step in range(1, self.cols_n):
+            src = self.block(ref, self.place(step, 1 - self.row), tokens)
+            self.near(phase, step, src, pair.at[step]).wait_recv()
+            mine = self.block(ref, self.place(step, self.row), tokens)
+            mine[...] = (mine[...].astype(F32) + pair[step].astype(F32)).astype(BF16)
+            self.far(phase, step, mine, landing.at[step - 1]).start()
+
+    def scatter_sum(self, phase, ref, pair, landing, tokens):
+        src = self.block(ref, self.place(0, 1 - self.row), tokens)
+        self.near(phase, 0, src, pair.at[0]).wait_recv()
+        total = self.block(ref, self.me, tokens)[...].astype(F32) + pair[0].astype(F32)
+        for step in range(1, self.cols_n):
+            mine = self.block(ref, self.place(step, self.row), tokens)
+            self.far(phase, step, mine, landing.at[step - 1]).wait_recv()
             total += landing[step - 1].astype(F32)
-            copy.wait_send()
+        for step in range(self.cols_n):
+            src = self.block(ref, self.place(step, 1 - self.row), tokens)
+            self.near(phase, step, src, pair.at[step]).wait_send()
+        for step in range(1, self.cols_n):
+            mine = self.block(ref, self.place(step, self.row), tokens)
+            self.far(phase, step, mine, landing.at[step - 1]).wait_send()
         return total
 
 
@@ -191,9 +233,9 @@
     rows_n, cols_n,
     x_ref, gain_a, gain_f, wqkv, wout, wgu, wdn, cos, sin, own_seg, own_tok, all_seg,
     y_ref, a_ref, qkv_ref, kv_ref, o_ref, r_ref, b_ref, gu_ref, hid_ref,
-    part, landing, send_sem, recv_sem,
+    part, pair, landing, *sems,
 ):
-    group = Group(rows_n, cols_n, send_sem, recv_sem)
+    group = Group(rows_n, cols_n, *sems)
     tokens, width = x_ref.shape
     kv_width = kv_ref.shape[1]
     ff = hid_ref.shape[1]
@@ -227,8 +269,9 @@
     gate = gu_ref[:, :ff]
     hid_ref[...] = (gate / (1.0 + jnp.exp(-gate)) * gu_ref[:, ff:]).astype(BF16)
     part[...] = dot(hid_ref[...], wdn[...]).astype(BF16)
-    group.scatter_start(2, part, landing, tokens)
-    y_ref[...] = r_ref[...] + group.scatter_sum(2, part, landing, tokens)
+    group.scatter_near(2, part, pair, tokens)
+    group.scatter_far(2, part, pair, landing, tokens)
+    y_ref[...] = r_ref[...] + group.scatter_sum(2, part, pair, landing, tokens)
 
 
 def norm_back(x, gain, gz):
@@ -246,10 +289,10 @@
     gy_ref, x_ref, gain_a, gain_f, wqkv, wout, wgu, wdn, cos, sin, own_seg, own_tok, all_seg,
     a_ref, qkv_ref, kv_ref, o_ref, r_ref, b_ref, gu_ref, hid_ref,
     gx_ref, gwqkv, gwout, gwgu, gwdn, ggain_a, ggain_f,
-    gf_ref, ggu_ref, part, landing, kv_part, kv_landing, go_ref, gq_ref, gr_ref,
-    send_sem, recv_sem,
+    gf_ref, ggu_ref, part, pair, landing, kv_part, kv_pair, kv_landing, go_ref, gq_ref, gr_ref,
+    *sems,
 ):
-    group = Group(rows_n, cols_n, send_sem, recv_sem)
+    group = Group(rows_n, cols_n, *sems)
     tokens, width = x_ref.shape
     kv_width = kv_ref.shape[1]
     half = kv_width // 2
@@ -264,10 +307,11 @@
     ggu_ref[:, :ff] = (ghid * gu_ref[:, ff:] * (sig * (1.0 + gate * (1.0 - sig)))).astype(BF16)
     ggu_ref[:, ff:] = (ghid * (gate * sig)).astype(BF16)
     part[...] = dot_nt(ggu_ref[...], wgu[...]).astype(BF16)
-    group.scatter_start(1, part, landing, tokens)
+    group.scatter_near(1, part, pair, tokens)
     gwdn[...] = dot_tn(hid_ref[...], gf_ref[...]).astype(BF16)
+    group.scatter_far(1, part, pair, landing, tokens)
     gwgu[...] = dot_tn(b_ref[...], ggu_ref[...]).astype(BF16)
-    gb = group.scatter_sum(1, part, landing, tokens)
+    gb = group.scatter_sum(1, part, pair, landing, tokens)
     grad, ggain_f[...] = norm_back(r_ref[...], gain_f[...], gb)
     gr = gy_ref[...] + grad
     gr_ref[...] = gr
@@ -291,9 +335,10 @@
         at = g * HEAD_DIM
         kv_part[:, at : at + HEAD_DIM] = (dot_tn(gs, queries) * factor).astype(BF16)
         kv_part[:, half + at : half + at + HEAD_DIM] = dot_tn(p.astype(BF16), gout).astype(BF16)
-    group.scatter_start(2, kv_part, kv_landing, tokens)
+    group.scatter_near(2, kv_part, kv_pair, tokens)
+    group.scatter_far(2, kv_part, kv_pair, kv_landing, tokens)
     gwout[...] = dot_tn(o_ref[...], gr_ref[...].astype(BF16)).astype(BF16)
-    gq_ref[:, :kv_width] = group.scatter_sum(2, kv_part, kv_landing, tokens)
+    gq_ref[:, :kv_width] = group.scatter_sum(2, kv_part, kv_pair, kv_landing, tokens)
     g0 = gq_ref[...]
     packed = (g0 * cos[...] - turned(g0 * sin[...])).astype(BF16)
     ga = dot_nt(packed, wqkv[...])
@@ -303,7 +348,6 @@
 
 
 def call_layer(body, operands, out_shapes, scratch, rows_n, cols_n, phases, collective_id, name):
-    size = rows_n * cols_n
     spec = pl.BlockSpec(memory_space=pltpu.VMEM)
     return pl.pallas_call(
         functools.partial(body, rows_n, cols_n),
@@ -311,7 +355,8 @@
         in_specs=[spec] * len(operands),
         out_specs=[spec] * len(out_shapes),
         scratch_shapes=[pltpu.VMEM(shape, kind) for shape, kind in scratch]
-        + [pltpu.SemaphoreType.DMA((phases, size - 1))] * 2,
+        + [pltpu.SemaphoreType.DMA((phases, cols_n - 1))] * 2
+        + [pltpu.SemaphoreType.DMA((phases, cols_n))] * 2,
         compiler_params=pltpu.CompilerParams(
             collective_id=collective_id, has_side_effects=True, vmem_limit_bytes=VMEM_LIMIT
         ),
@@ -358,19 +403,34 @@
     ).transpose(1, 0, 2, 3).reshape(rows_n, band, 2 * fc)
     down = w_down[0].reshape(rows_n, fc, band)
     gains = jnp.stack([gain_attn[0], gain_ffn[0]])
-    qkv, out, gate_up, down, gains = exchange(
-        [(qkv, True), (w_out[0], True), (gate_up, True), (down, True), (gains, True)], "section", 0
-    )
-    qkv, out = exchange([(qkv, True), (out, True)], "col", 1)
+    own_qkv, own_out, qkv, out, gate_up, down, gains = exchange(
+        [
+            (qkv, "col", True), (w_out[0], "col", True),
+            (qkv, "section", True), (w_out[0], "section", True), (gate_up, "section", True),
+            (down, "section", True), (gains, "section", True),
+        ],
+        0,
+    )
+
+    def other(item):
+        return lax.dynamic_index_in_dim(item, 1 - section, 0, False)
+
+    def in_order(own, theirs):
+        first = section == 0
+        return jnp.stack([jnp.where(first, own, theirs), jnp.where(first, theirs, own)], axis=1)
+
+    qkv, out = exchange([(other(qkv), "col", True), (other(out), "col", True)], 1)
+    qkv, out = in_order(own_qkv, qkv), in_order(own_out, out)
     mine = lax.dynamic_index_in_dim(inputs[0], section, 0, False).reshape(rows_n, tokens, band)
     cot = lax.dynamic_index_in_dim(cotangent[0], section, 0, False).reshape(rows_n, tokens, band)
     qkv, out, gate_up, down, gains, mine, cot = exchange(
         [
-            (qkv, True), (out, True),
-            (gate_up.transpose(1, 0, 2, 3), False), (down.transpose(1, 0, 2, 3), False),
-            (gains, True), (mine, False), (cot, False),
+            (qkv, "row", True), (out, "row", True),
+            (gate_up.transpose(1, 0, 2, 3), "row", False),
+            (down.transpose(1, 0, 2, 3), "row", False),
+            (gains, "row", True), (mine, "row", False), (cot, "row", False),
         ],
-        "row", 2,
+        2,
     )
     layers = gains.shape[1]
     pad = jnp.zeros((width, padded - used), BF16)
@@ -414,7 +474,10 @@
                 ((length, kv_width), BF16), ((tokens, width), BF16), ((tokens, width), F32),
                 ((length, width), BF16), ((length, 2 * fp), F32), ((length, fp), BF16),
             ],
-            [((length, width), BF16), ((size - 1, tokens, width), BF16)],
+            [
+                ((length, width), BF16), ((cols_n, tokens, width), BF16),
+                ((cols_n - 1, tokens, width), BF16),
+            ],
             rows_n, cols_n, 3, 3, "layer_forward",
         )
         saved.append((entry, kept))
@@ -434,8 +497,9 @@
             ],
             [
                 ((length, width), BF16), ((length, 2 * fp), BF16), ((length, width), BF16),
-                ((size - 1, tokens, width), BF16), ((length, kv_width), BF16),
-                ((size - 1, tokens, kv_width), BF16), ((tokens, width), BF16),
+                ((cols_n, tokens, width), BF16), ((cols_n - 1, tokens, width), BF16),
+                ((length, kv_width), BF16), ((cols_n, tokens, kv_width), BF16),
+                ((cols_n - 1, tokens, kv_width), BF16), ((tokens, width), BF16),
                 ((tokens, padded), F32), ((tokens, width), F32),
             ],
             rows_n, cols_n, 3, 4, "layer_backward",
@@ -475,36 +539,42 @@
     act = jnp.stack(acts).reshape(layers, tokens, rows_n, band).transpose(2, 0, 1, 3)
     in_grad = jnp.stack(grads).reshape(layers, tokens, rows_n, band).transpose(2, 0, 1, 3)
     g_qkv, g_out, g_gu, g_dn, g_gain, act, in_grad = exchange(
-        [(item, False) for item in (g_qkv, g_out, g_gu, g_dn, g_gain, act, in_grad)], "row", 5
+        [(item, "row", False) for item in (g_qkv, g_out, g_gu, g_dn, g_gain, act, in_grad)], 5
     )
 
     def add(item):
         return jnp.sum(item.astype(F32), axis=0)
 
-    g_qkv, g_out, g_gu, g_dn, g_gain, act, in_grad = exchange(
+    g_qkv, g_out, g_gain = exchange(
         [
-            (add(g_qkv).astype(BF16), False), (add(g_out).astype(BF16), False),
-            (g_gu.transpose(1, 0, 2, 3), False), (g_dn.transpose(1, 0, 2, 3), False),
-            (add(g_gain), False),
-            (act.transpose(1, 0, 2, 3), False), (in_grad.transpose(1, 0, 2, 3), False),
+            (add(g_qkv).astype(BF16), "section", False),
+            (add(g_out).astype(BF16), "section", False),
+            (add(g_gain), "section", False),
         ],
-        "section", 6,
+        6,
+    )
+    g_qkv, g_out, g_gain, g_gu, g_dn, act, in_grad = exchange(
+        [
+            (add(g_qkv).astype(BF16), "col", False), (add(g_out).astype(BF16), "col", False),
+            (add(g_gain), "col", True),
+            (g_gu.transpose(1, 0, 2, 3), "section", False),
+            (g_dn.transpose(1, 0, 2, 3), "section", False),
+            (act.transpose(1, 0, 2, 3), "section", False),
+            (in_grad.transpose(1, 0, 2, 3), "section", False),
+        ],
+        7,
     )
     activations = act.reshape((1, 1) + inputs.shape[1:])
     input_grads = in_grad.reshape((1, 1) + inputs.shape[1:])
-    g_qkv, g_out, g_gain = exchange(
-        [(add(g_qkv).astype(BF16), False), (add(g_out).astype(BF16), False), (add(g_gain), True)],
-        "col", 7,
-    )
     g_qkv, g_out, g_gu, g_dn, g_gain = (
         add(item)
         for item in exchange(
             [
-                (add(g_qkv).astype(BF16), True), (add(g_out).astype(BF16), True),
-                (add(g_gu).astype(BF16), True), (add(g_dn).astype(BF16), True),
-                (add(g_gain), True),
+                (add(g_qkv).astype(BF16), "dp", True), (add(g_out).astype(BF16), "dp", True),
+                (add(g_gu).astype(BF16), "dp", True), (add(g_dn).astype(BF16), "dp", True),
+                (add(g_gain), "dp", True),
             ],
-            "dp", 8,
+            8,
         )
     )
     g_gu = g_gu.reshape(rows_n, band, 2, fc).transpose(2, 1, 0, 3).reshape(2, band, rows_n * fc)

time: 707 us -> 428 us (0.61); the launches traced: 695 us -> 423 us
  Pallas kernels: 583 us -> 307 us
    pallas_call x7, Pallas kernels: 379 us -> 162 us  [exchange(): pl.pallas_call(body, out_shape=shapes, in_specs=[spec] * count, out_specs...]
    pallas_call x4, Pallas kernels: 204 us -> 144 us  [call_layer(): pl.pallas_call(functools.partial(body, rows_n, cols_n), out_shape=[jax.Sh...]
where the time goes in v2:
time: 428 us; the launch traced here: 423 us
  Pallas kernels  307 us (72%)
  local copies, waits for them, and re-layouts  72.6 us (17%)
  other arithmetic  41.6 us (10%)
    pallas_call x7, Pallas kernels, exchange(): pl.pallas_call(body, out_shape=shapes, in_specs=[spec] * count, out_specs...  162 us
    pallas_call x4, Pallas kernels, call_layer(): pl.pallas_call(functools.partial(body, rows_n, cols_n), out_shape=[jax.Sh...  144 us
    reduce_sum x16, other arithmetic, add(): return jnp.sum(item.astype(F32), axis=0)  17.7 us
    unnamed x122, local copies, waits for them, and re-layouts  11.5 us

profile of v2, /device:TPU:0, one launch (start us, length us, event | category | flops | bytes accessed | tf_op | source)
XLA Modules:
  0.0 422.8 jit_solution(327882770940860498)
XLA Ops:
  0.7 1.2 stack_reshape_squeeze.6
  3.0 1.5 maximum_bitcast_fusion.2
  4.5 1.1 reshape.280.refs_4_
  6.8 0.9 copy.264
  8.3 31.7 %exchange_0.1 = (bf16[4,288,240]{2,1,0:T(8,128)(2,1)}, bf16[4,144,288]{2,1,0:T(8,128)(2,1)}, bf16[2,288,240]{2,1,0:T(8,128)(2,1)}, bf16[2,144,288]{2,1,0:T(8,128...) custom-call(bf16[288,240]{1,0:T(8,128)(2,1)} %pad_maximum_fusion.6.refs_0_.re, ...), custom_call_target="tpu_custom_call" | custom-call | tf_op jit(solution)/shard_map/exchange_0/pallas_call | solution.py:90
  40.0 1.6 dynamic-slice_bitcast_fusion.refs_0_
  41.6 1.6 dynamic-slice_bitcast_fusion.1.refs_1_
  43.2 25.3 %exchange_1.1 = (bf16[4,288,240]{2,1,0:T(8,128)(2,1)}, bf16[4,144,288]{2,1,0:T(8,128)(2,1)}) custom-call(bf16[288,240]{1,0:T(8,128)(2,1)} %dynamic-slice_bitcast_fusion.refs_0_, bf16[144,288]{1,0:T(8,128)(2,1)} %dynamic-slice_bitcast_fusion.1.refs_1_), custom_call_target="tpu_custom_call" | custom-call | tf_op jit(solution)/shard_map/exchange_1/pallas_call | solution.py:90
  68.5 1.2 select_bitcast_fusion.3
  69.8 1.1 pad_maximum_fusion.3.refs_1_
  71.5 1.2 pad_maximum_fusion.2.refs_0_
  74.2 1.0 copy.370
  75.2 0.9 copy.372
  76.1 10.1 %exchange_2.1 = (bf16[2,4,2,288,240]{4,3,2,1,0:T(8,128)(2,1)}, bf16[2,4,2,144,288]{4,3,2,1,0:T(8,128)(2,1)}, bf16[2,2,288,384]{3,2,1,0:T(8,128)(2,1)}, bf16[2,2,...) custom-call(bf16[4,2,288,240]{3,2,1,0:T(8,128)(2,1)} %pad_maximum_fu, ...), custom_call_target="tpu_custom_call" | custom-call | tf_op jit(solution)/shard_map/exchange_2/pallas_call | solution.py:90
  86.2 1.8 slice_bitcast_fusion
  88.6 1.0 reshape.314
  89.9 1.0 reshape.315
  91.6 1.0 reshape.317
  92.9 1.0 reshape.318
  94.5 0.9 copy.333
  96.6 0.9 copy.336
  98.6 3.3 maximum_maximum_fusion.1
  103.3 1.6 slice_bitcast_fusion.2
  104.9 0.9 copy.279
  105.8 1.5 reshape.286.wout
  108.3 0.9 copy.355
  115.8 35.6 %layer_forward.2 = (f32[64,576]{1,0:T(8,128)}, bf16[64,576]{1,0:T(8,128)(2,1)}, bf16[64,1024]{1,0:T(8,128)(2,1)}, bf16[512,384]{1,0:T(8,128)(2,1)}, bf16[64,576]...) custom-call(f32[64,576]{1,0:T(8,128)} %reshape.311.x_ref, ...), custom_call_target="tpu_custom_call" | custom-call | tf_op jit(solution)/shard_map/layer_forward/pallas_call | solution.py:352
  151.3 1.6 fusion.3
  154.2 0.9 copy.291
  155.2 1.5 reshape.292.wout
  157.5 1.0 copy.356
  159.8 35.5 %layer_forward.3 = (f32[64,576]{1,0:T(8,128)}, bf16[64,576]{1,0:T(8,128)(2,1)}, bf16[64,1024]{1,0:T(8,128)(2,1)}, bf16[512,384]{1,0:T(8,128)(2,1)}, bf16[64,576]...) custom-call(f32[64,576]{1,0:T(8,128)} %get-tuple-element.210.x_ref, ...), custom_call_target="tpu_custom_call" | custom-call | tf_op jit(solution)/shard_map/layer_forward/pallas_call | solution.py:352
  196.4 36.7 %layer_backward.2 = (f32[64,576]{1,0:T(8,128)}, bf16[576,1024]{1,0:T(8,128)(2,1)}, bf16[576,576]{1,0:T(8,128)(2,1)}, bf16[576,512]{1,0:T(8,128)(2,1)}, bf16[256,...) custom-call(f32[64,576]{1,0:T(8,128)} %reshape.310.gy_ref, f32[64,576]{1,0:T(8,128)} %get-tuple-element.210.x_ref, ...), custom_call_target="tpu_custom_call" | custom-call | tf_op jit(solution)/shard_map/layer_backward/pallas_call | solution.py:352
  233.0 1.6 convert_convert_fusion.gy_ref
  234.6 36.5 %layer_backward.3 = (f32[64,576]{1,0:T(8,128)}, bf16[576,1024]{1,0:T(8,128)(2,1)}, bf16[576,576]{1,0:T(8,128)(2,1)}, bf16[576,512]{1,0:T(8,128)(2,1)}, bf16[256,...) custom-call(f32[64,576]{1,0:T(8,128)} %convert_convert_fusion.gy_ref, f32[64,576]{1,0:T(8,128)} %reshape.311.x_ref, ...), custom_call_target="tpu_custom_call" | custom-call | tf_op jit(solution)/shard_map/layer_backward/pallas_call | solution.py:352
  271.2 1.1 stack.121
  276.3 0.9 pad_maximum_fusion.5.refs_3_
  278.7 1.0 pad_maximum_fusion.4.refs_2_
  282.7 1.5 pad_maximum_fusion.1.refs_1_
  286.3 1.1 maximum_bitcast_fusion
  288.6 1.1 copy-done.4
  289.7 0.9 fusion.6
  291.0 1.3 reshape.324
  292.3 1.1 maximum_bitcast_fusion.1
  293.4 1.9 pad_maximum_fusion.refs_0_
  295.3 11.1 %exchange_5.1 = (bf16[2,2,4,288,240]{4,3,2,1,0:T(8,128)(2,1)}, bf16[2,2,4,144,288]{4,3,2,1,0:T(8,128)(2,1)}, bf16[2,2,288,384]{3,2,1,0:T(8,128)(2,1)}, bf16[2,2,...) custom-call(bf16[2,2,4,288,240]{4,3,2,1,0:T(8,128)(2,1)} %pad_maximu, ...), custom_call_target="tpu_custom_call" | custom-call | tf_op jit(solution)/shard_map/exchange_5/pallas_call | solution.py:90
  306.4 3.6 reduce_sum.178.refs_0_
  310.0 1.6 reduce_sum.179.refs_1_
  312.2 27.9 %exchange_6.1 = (bf16[2,4,288,240]{3,2,1,0:T(8,128)(2,1)}, bf16[2,4,144,288]{3,2,1,0:T(8,128)(2,1)}, f32[2,2,288]{2,1,0:T(2,128)}) custom-call(bf16[2,4,288,240]{3,2,1,0:T(8,128)(2,1)} %reduce_sum.178.refs_0_, bf16[2,4,144,288]{3,2,1,0:T(8,128)(2,1)} %reduce_sum.179.refs_1_, f32[2,2,288]{2,1,0:T(2,128)} %reduce_sum.180.refs_2_), custom_call_target="tpu_custom_call" | custom-call | tf_op jit(solution)/shard_map/exchange_6/pallas_call | solution.py:90
  340.1 2.6 reduce_sum.181.refs_0_
  342.7 1.1 reduce_sum.182.refs_1_
  344.4 1.0 copy.367
  345.4 0.9 copy.371
  347.8 30.4 %exchange_7.1 = (bf16[4,288,240]{2,1,0:T(8,128)(2,1)}, bf16[4,144,288]{2,1,0:T(8,128)(2,1)}, f32[4,2,288]{2,1,0:T(2,128)}, bf16[2,2,288,384]{3,2,1,0:T(8,128)(2,...) custom-call(bf16[4,288,240]{2,1,0:T(8,128)(2,1)} %reduce_sum.181.refs_0_, ...), custom_call_target="tpu_custom_call" | custom-call | tf_op jit(solution)/shard_map/exchange_7/pallas_call | solution.py:90
  378.2 2.3 reduce_sum.186.refs_2_
  380.5 0.9 reduce_sum.187.refs_3_
  383.6 25.7 %exchange_8.1 = (bf16[2,288,240]{2,1,0:T(8,128)(2,1)}, bf16[2,144,288]{2,1,0:T(8,128)(2,1)}, bf16[2,2,288,384]{3,2,1,0:T(8,128)(2,1)}, bf16[2,2,192,288]{3,2,1,0:T(8,128)(2,1)}, f32[2,2,288]{2,1,0:T(2,128)}) custom-call(bf16[288,240]{1,0:T(8,128)(2,1)} %reduce_sum.184.refs_0_, bf16[144,288]{1,0:T(8,128)(2,1)} %reduce_sum.185.refs_1_, ...), custom_call_target="tpu_custom_call" | custom-call | tf_op jit(solution)/shard_map/exchange_8/pallas_call | solution.py:90
  409.3 1.4 convert_reduce_fusion
  410.7 0.8 reshape.309
  411.6 0.9 fusion.4
  413.0 1.2 slice.157
  414.7 1.2 slice.159
  416.0 1.0 copy.330
  420.9 0.9 copy.326
  (242 shorter events, 45.1 us)
Async XLA Ops:
  0.6 111.2 %copy-start = (s32[1,2,512]{2,1,0:T(2,128)S(1)}, s32[1,2,512]{2,1,0:T(2,128)}, u32[]{:S(2)}) copy-start(s32[1,2,512]{2,1,0:T(2,128)} %param.13) | copy-start | bytes 12292
  0.7 1.7 copy-start.30
  3.0 2.6 copy-start.37
  3.0 2.7 copy-start.40
  3.0 2.8 copy-start.41
  4.5 2.3 copy-start.31
  4.5 3.2 copy-start.53
  4.5 3.2 copy-start.54
  69.8 1.1 copy-start.15
  69.8 1.6 copy-start.16
  71.4 1.2 copy-start.42
  71.4 1.2 copy-start.43
  71.4 2.7 copy-start.9
  72.7 2.5 copy-start.20
  97.5 1.0 copy-start.6
  97.6 1.0 copy-start.7
  98.6 3.3 copy-start.48
  105.8 1.5 copy-start.8
  107.8 1.5 copy-start.18
  109.2 1.4 copy-start.39
  159.8 35.5 %copy-start.38 = (bf16[2,64,288]{2,1,0:T(8,128)(2,1)S(1)}, bf16[2,64,288]{2,1,0:T(8,128)(2,1)}, u32[]{:S(2)}) copy-start(bf16[2,64,288]{2,1,0:T(8,128)(2,1)} %get-tuple-element.90) | copy-start | bytes 221188
  234.6 37.7 %copy-start.14 = (f32[64,576]{1,0:T(8,128)S(1)}, f32[64,576]{1,0:T(8,128)}, u32[]{:S(2)}) copy-start(f32[64,576]{1,0:T(8,128)} %get-tuple-element.106) | copy-start | bytes 442372
  271.2 2.2 copy-start.36
  272.6 1.9 copy-start.52
  272.6 2.0 copy-start.51
  272.6 2.1 copy-start.50
  272.6 2.2 copy-start.49
  272.6 2.9 copy-start.35
  273.7 2.1 copy-start.34
  275.9 1.3 copy-start.19
  277.2 1.1 copy-start.17
  278.4 1.4 copy-start.13
  280.6 1.1 copy-start.12
  282.7 1.5 copy-start.5
  286.3 1.3 copy-start.3
  288.4 1.3 copy-start.4
  306.4 3.6 copy-start.2
  310.0 1.6 copy-start.44
  340.1 2.6 copy-start.11
  340.1 3.7 copy-start.47
  340.1 4.3 %copy-start.10 = (bf16[2,2,288,384]{3,2,1,0:T(8,128)(2,1)S(1)}, bf16[2,2,288,384]{3,2,1,0:T(8,128)(2,1)}, u32[]{:S(2)}) copy-start(bf16[2,2,288,384]{3,2,1,0:T(8,128)(2,1)} %get-tuple-element.135) | copy-start | bytes 2654212
  343.8 1.6 copy-start.21
  344.4 1.9 copy-start.26
  345.4 1.7 copy-start.32
  378.2 2.3 copy-start.24
  378.2 3.3 copy-start.23
  378.2 4.0 copy-start.25
  380.5 2.5 copy-start.45
  414.2 1.7 copy-start.22
  415.9 1.1 copy-start.28
  417.0 2.6 copy-start.29
  417.0 3.3 copy-start.46
  417.0 3.9 copy-start.27
  417.2 5.4 %copy-start.1 = (s32[1,2,512]{2,1,0:T(2,128)S(1)}, s32[1,2,512]{2,1,0:T(2,128)}, u32[]{:S(2)}) copy-start(s32[1,2,512]{2,1,0:T(2,128)} %param.13) | copy-start | bytes 12292
  418.0 3.8 copy-start.33

commit v3 on v2

--- a/solution.py
+++ b/solution.py
@@ -545,20 +545,27 @@
     def add(item):
         return jnp.sum(item.astype(F32), axis=0)
 
-    g_qkv, g_out, g_gain = exchange(
+    def of_layer(item, layer):
+        return lax.dynamic_index_in_dim(item, layer, 1, False)
+
+    g_qkv, g_out, g_gain, sent_gu, sent_dn = exchange(
         [
             (add(g_qkv).astype(BF16), "section", False),
             (add(g_out).astype(BF16), "section", False),
             (add(g_gain), "section", False),
+            (of_layer(g_gu, 1 - section), "dp", True),
+            (of_layer(g_dn, 1 - section), "dp", True),
         ],
         6,
     )
-    g_qkv, g_out, g_gain, g_gu, g_dn, act, in_grad = exchange(
+    g_qkv, g_out, g_gain, came_gu, came_dn, g_gu, g_dn, act, in_grad = exchange(
         [
             (add(g_qkv).astype(BF16), "col", False), (add(g_out).astype(BF16), "col", False),
             (add(g_gain), "col", True),
-            (g_gu.transpose(1, 0, 2, 3), "section", False),
-            (g_dn.transpose(1, 0, 2, 3), "section", False),
+            (add(sent_gu).astype(BF16), "section", True),
+            (add(sent_dn).astype(BF16), "section", True),
+            (of_layer(g_gu, section), "dp", True),
+            (of_layer(g_dn, section), "dp", True),
             (act.transpose(1, 0, 2, 3), "section", False),
             (in_grad.transpose(1, 0, 2, 3), "section", False),
         ],
@@ -566,12 +573,13 @@
     )
     activations = act.reshape((1, 1) + inputs.shape[1:])
     input_grads = in_grad.reshape((1, 1) + inputs.shape[1:])
-    g_qkv, g_out, g_gu, g_dn, g_gain = (
+    g_gu = add(g_gu) + other(came_gu).astype(F32)
+    g_dn = add(g_dn) + other(came_dn).astype(F32)
+    g_qkv, g_out, g_gain = (
         add(item)
         for item in exchange(
             [
                 (add(g_qkv).astype(BF16), "dp", True), (add(g_out).astype(BF16), "dp", True),
-                (add(g_gu).astype(BF16), "dp", True), (add(g_dn).astype(BF16), "dp", True),
                 (add(g_gain), "dp", True),
             ],
             8,

time: 428 us -> 414 us (0.967)
  Pallas kernels: 307 us -> 291 us
    pallas_call x7, Pallas kernels: 162 us -> 147 us  [exchange(): pl.pallas_call(body, out_shape=shapes, in_specs=[spec] * count, out_specs...]
    unnamed x122 -> x125, local copies, waits for them, and re-layouts: 11.5 us -> 12 us
where the time goes in v3:
time: 414 us; the launch traced here: 409 us
  Pallas kernels  291 us (70%)
  local copies, waits for them, and re-layouts  73.1 us (18%)
  other arithmetic  41.9 us (10%)
    pallas_call x7, Pallas kernels, exchange(): pl.pallas_call(body, out_shape=shapes, in_specs=[spec] * count, out_specs...  147 us
    pallas_call x4, Pallas kernels, call_layer(): pl.pallas_call(functools.partial(body, rows_n, cols_n), out_shape=[jax.Sh...  144 us
    reduce_sum x16, other arithmetic, add(): return jnp.sum(item.astype(F32), axis=0)  17.4 us
    unnamed x125, local copies, waits for them, and re-layouts  12 us

profile of v3, /device:TPU:0, one launch (start us, length us, event | category | flops | bytes accessed | tf_op | source)
XLA Modules:
  0.0 408.8 jit_solution(841840647395242080)
XLA Ops:
  0.7 1.2 stack_reshape_squeeze.6
  3.0 1.5 maximum_bitcast_fusion.2
  4.5 1.1 reshape.304.refs_4_
  6.8 0.9 copy.197
  8.3 31.8 %exchange_0.1 = (bf16[4,288,240]{2,1,0:T(8,128)(2,1)}, bf16[4,144,288]{2,1,0:T(8,128)(2,1)}, bf16[2,288,240]{2,1,0:T(8,128)(2,1)}, bf16[2,144,288]{2,1,0:T(8,128...) custom-call(bf16[288,240]{1,0:T(8,128)(2,1)} %pad_maximum_fusion.6.refs_0_.re, ...), custom_call_target="tpu_custom_call" | custom-call | tf_op jit(solution)/shard_map/exchange_0/pallas_call | solution.py:90
  40.1 1.6 dynamic-slice_bitcast_fusion.4.refs_0_
  41.7 1.6 dynamic-slice_bitcast_fusion.5.refs_1_
  43.2 25.3 %exchange_1.1 = (bf16[4,288,240]{2,1,0:T(8,128)(2,1)}, bf16[4,144,288]{2,1,0:T(8,128)(2,1)}) custom-call(bf16[288,240]{1,0:T(8,128)(2,1)} %dynamic-slice_bitcast_fusion.4.refs_0_, bf16[144,288]{1,0:T(8,128)(2,1)} %dynamic-slice_bitcast_fusion.5.refs_1_), custom_call_target="tpu_custom_call" | custom-call | tf_op jit(solution)/shard_map/exchange_1/pallas_call | solution.py:90
  68.5 1.2 select_bitcast_fusion.3
  69.8 1.1 pad_maximum_fusion.3.refs_1_
  71.5 1.2 pad_maximum_fusion.2.refs_0_
  74.3 1.0 copy.299
  75.3 0.9 copy.300
  76.2 10.1 %exchange_2.1 = (bf16[2,4,2,288,240]{4,3,2,1,0:T(8,128)(2,1)}, bf16[2,4,2,144,288]{4,3,2,1,0:T(8,128)(2,1)}, bf16[2,2,288,384]{3,2,1,0:T(8,128)(2,1)}, bf16[2,2,...) custom-call(bf16[4,2,288,240]{3,2,1,0:T(8,128)(2,1)} %pad_maximum_fu, ...), custom_call_target="tpu_custom_call" | custom-call | tf_op jit(solution)/shard_map/exchange_2/pallas_call | solution.py:90
  86.4 1.8 slice_bitcast_fusion
  88.6 0.9 copy.265
  89.5 1.7 reshape.341
  91.7 0.9 copy.268
  92.6 1.6 reshape.344
  98.1 2.2 maximum_maximum_fusion.1
  100.5 0.9 copy.212
  101.5 1.5 reshape.310.wout
  104.0 0.9 copy.287
  106.5 1.2 reshape.334.x_ref
  113.0 35.5 %layer_forward.2 = (f32[64,576]{1,0:T(8,128)}, bf16[64,576]{1,0:T(8,128)(2,1)}, bf16[64,1024]{1,0:T(8,128)(2,1)}, bf16[512,384]{1,0:T(8,128)(2,1)}, bf16[64,576]...) custom-call(f32[64,576]{1,0:T(8,128)} %reshape.334.x_ref, ...), custom_call_target="tpu_custom_call" | custom-call | tf_op jit(solution)/shard_map/layer_forward/pallas_call | solution.py:352
  148.6 1.6 fusion.3
  150.2 0.9 copy.224
  151.1 1.5 reshape.316.wout
  153.4 0.9 copy.288
  157.1 35.5 %layer_forward.3 = (f32[64,576]{1,0:T(8,128)}, bf16[64,576]{1,0:T(8,128)(2,1)}, bf16[64,1024]{1,0:T(8,128)(2,1)}, bf16[512,384]{1,0:T(8,128)(2,1)}, bf16[64,576]...) custom-call(f32[64,576]{1,0:T(8,128)} %get-tuple-element.203.x_ref, ...), custom_call_target="tpu_custom_call" | custom-call | tf_op jit(solution)/shard_map/layer_forward/pallas_call | solution.py:352
  193.6 36.6 %layer_backward.2 = (f32[64,576]{1,0:T(8,128)}, bf16[576,1024]{1,0:T(8,128)(2,1)}, bf16[576,576]{1,0:T(8,128)(2,1)}, bf16[576,512]{1,0:T(8,128)(2,1)}, bf16[256,...) custom-call(f32[64,576]{1,0:T(8,128)} %reshape.333.gy_ref, f32[64,576]{1,0:T(8,128)} %get-tuple-element.203.x_ref, ...), custom_call_target="tpu_custom_call" | custom-call | tf_op jit(solution)/shard_map/layer_backward/pallas_call | solution.py:352
  230.2 1.6 convert_convert_fusion.gy_ref
  231.8 36.5 %layer_backward.3 = (f32[64,576]{1,0:T(8,128)}, bf16[576,1024]{1,0:T(8,128)(2,1)}, bf16[576,576]{1,0:T(8,128)(2,1)}, bf16[576,512]{1,0:T(8,128)(2,1)}, bf16[256,...) custom-call(f32[64,576]{1,0:T(8,128)} %convert_convert_fusion.gy_ref, f32[64,576]{1,0:T(8,128)} %reshape.334.x_ref, ...), custom_call_target="tpu_custom_call" | custom-call | tf_op jit(solution)/shard_map/layer_backward/pallas_call | solution.py:352
  268.3 1.1 stack.121
  273.4 0.9 pad_maximum_fusion.5.refs_3_
  275.9 1.1 pad_maximum_fusion.4.refs_2_
  279.8 1.6 pad_maximum_fusion.1.refs_1_
  283.4 1.1 maximum_bitcast_fusion
  285.7 1.1 copy-done.7
  286.8 0.9 fusion.6
  288.1 1.3 reshape.349
  289.5 1.1 maximum_bitcast_fusion.1
  290.6 2.0 pad_maximum_fusion.refs_0_
  292.5 11.3 %exchange_5.1 = (bf16[2,2,4,288,240]{4,3,2,1,0:T(8,128)(2,1)}, bf16[2,2,4,144,288]{4,3,2,1,0:T(8,128)(2,1)}, bf16[2,2,288,384]{3,2,1,0:T(8,128)(2,1)}, bf16[2,2,...) custom-call(bf16[2,2,4,288,240]{4,3,2,1,0:T(8,128)(2,1)} %pad_maximu, ...), custom_call_target="tpu_custom_call" | custom-call | tf_op jit(solution)/shard_map/exchange_5/pallas_call | solution.py:90
  303.8 3.6 reduce_sum.182.refs_0_
  307.4 1.0 dynamic-slice_bitcast_fusion
  309.2 1.6 reduce_sum.183.refs_1_
  310.8 0.9 dynamic-slice_bitcast_fusion.2
  312.3 29.6 %exchange_6.1 = (bf16[2,4,288,240]{3,2,1,0:T(8,128)(2,1)}, bf16[2,4,144,288]{3,2,1,0:T(8,128)(2,1)}, f32[2,2,288]{2,1,0:T(2,128)}, bf16[2,2,288,384]{3,2,1,0:T(8,128)(2,1)}, bf16[2,2,192,288]{3,2,1,0:T(8,128)(2,1)}) custom-call(bf16[2,4,288,240]{3,2,1,0:T(8,128)(2,1)} %reduce_sum.182.refs_0_, bf16[2,4,144,288]{3,2,1,0:T(8,128)(2,1)} %reduce_sum.183.refs_1_, ...), custom_call_target="tpu_custom_call" | custom-call | tf_op jit(solution)/shard_map/exchange_6/pallas_call | solution.py:90
  341.9 2.6 reduce_sum.185.refs_0_
  344.5 1.1 reduce_sum.186.refs_1_
  345.6 1.0 reduce_sum.188.refs_3_
  346.7 0.9 reduce_sum.189.refs_4_
  349.6 30.4 %exchange_7.1 = (bf16[4,288,240]{2,1,0:T(8,128)(2,1)}, bf16[4,144,288]{2,1,0:T(8,128)(2,1)}, f32[4,2,288]{2,1,0:T(2,128)}, bf16[2,2,288,384]{3,2,1,0:T(8,128)(2,...) custom-call(bf16[4,288,240]{2,1,0:T(8,128)(2,1)} %reduce_sum.185.ref, ...), custom_call_target="tpu_custom_call" | custom-call | tf_op jit(solution)/shard_map/exchange_7/pallas_call | solution.py:90
  380.0 1.1 constant_dynamic-slice_fusion
  382.7 0.8 reshape.335
  383.6 1.4 convert_reduce_fusion
  385.0 0.8 reduce_sum.197
  386.4 0.9 fusion.4
  387.8 1.2 slice.157
  389.5 1.2 slice.159
  392.8 8.9 %exchange_8.1 = (bf16[2,288,240]{2,1,0:T(8,128)(2,1)}, bf16[2,144,288]{2,1,0:T(8,128)(2,1)}, f32[2,2,288]{2,1,0:T(2,128)}) custom-call(bf16[288,240]{1,0:T(8,128)(2,1)} %reduce_sum.190.refs_0_, bf16[144,288]{1,0:T(8,128)(2,1)} %reduce_sum.191.refs_1_, f32[2,288]{1,0:T(2,128)} %reduce_sum.192.refs_2_), custom_call_target="tpu_custom_call" | custom-call | tf_op jit(solution)/shard_map/exchange_8/pallas_call | solution.py:90
  401.7 1.0 convert_reduce_fusion.2
  406.6 0.9 copy.259
  (253 shorter events, 47.3 us)
Async XLA Ops:
  0.6 108.4 %copy-start = (s32[1,2,512]{2,1,0:T(2,128)S(1)}, s32[1,2,512]{2,1,0:T(2,128)}, u32[]{:S(2)}) copy-start(s32[1,2,512]{2,1,0:T(2,128)} %param.13) | copy-start | bytes 12292
  0.7 1.7 copy-start.32
  3.0 2.6 copy-start.39
  3.0 2.7 copy-start.42
  3.0 2.8 copy-start.43
  4.5 2.3 copy-start.33
  4.5 3.2 copy-start.55
  4.5 3.2 copy-start.56
  69.8 1.1 copy-start.17
  69.8 1.6 copy-start.18
  71.4 1.3 copy-start.44
  71.4 1.3 copy-start.45
  71.5 2.8 copy-start.10
  72.7 2.6 copy-start.22
  96.8 1.1 copy-start.2
  96.8 1.3 copy-start.3
  98.1 2.2 copy-start.4
  101.5 1.5 copy-start.9
  103.4 1.5 copy-start.21
  104.9 1.4 copy-start.41
  105.3 2.4 copy-start.50
  157.1 35.5 %copy-start.40 = (bf16[2,64,288]{2,1,0:T(8,128)(2,1)S(1)}, bf16[2,64,288]{2,1,0:T(8,128)(2,1)}, u32[]{:S(2)}) copy-start(bf16[2,64,288]{2,1,0:T(8,128)(2,1)} %get-tuple-element.92) | copy-start | bytes 221188
  231.8 37.7 %copy-start.16 = (f32[64,576]{1,0:T(8,128)S(1)}, f32[64,576]{1,0:T(8,128)}, u32[]{:S(2)}) copy-start(f32[64,576]{1,0:T(8,128)} %get-tuple-element.108) | copy-start | bytes 442372
  268.3 2.2 copy-start.38
  269.7 1.9 copy-start.54
  269.7 2.0 copy-start.53
  269.7 2.1 copy-start.52
  269.7 2.2 copy-start.51
  269.7 2.9 copy-start.37
  270.9 2.1 copy-start.36
  273.0 1.3 copy-start.20
  274.3 1.1 copy-start.19
  275.5 1.4 copy-start.15
  277.8 1.1 copy-start.14
  279.8 1.6 copy-start.8
  283.4 1.3 copy-start.6
  285.5 1.3 copy-start.7
  303.8 3.6 copy-start.11
  307.4 1.8 copy-start.5
  309.2 1.6 copy-start.26
  310.8 0.9 copy-start.46
  341.9 2.6 copy-start.13
  341.9 3.7 copy-start.12
  344.5 2.1 copy-start.25
  345.6 2.0 copy-start.49
  345.6 2.6 copy-start.28
  345.6 3.3 copy-start.34
  380.0 1.4 copy-start.24
  381.5 1.2 copy-start.30
  389.0 1.7 copy-start.23
  389.5 2.0 copy-start.27
  389.5 2.7 copy-start.47
  402.7 2.6 copy-start.31
  402.7 3.3 copy-start.48
  402.7 3.9 copy-start.29
  402.9 5.4 %copy-start.1 = (s32[1,2,512]{2,1,0:T(2,128)S(1)}, s32[1,2,512]{2,1,0:T(2,128)}, u32[]{:S(2)}) copy-start(s32[1,2,512]{2,1,0:T(2,128)} %param.13) | copy-start | bytes 12292
  403.7 3.8 copy-start.35
